TPU v7x, 32 devices: a whole 2x2x4 slice. The times are simulated.
32 devices in a mesh: dom: 2 (over y), blk: 4 (over z), sub: 2 (over x), rep: 2 (over core).
Axes of the slice: x: 2, y: 2, z: 4, core: 2. Of those that a mesh axis runs over, the one named last changes fastest.
Arguments:
- tokens: bfloat16 [4096, 2048], P(('dom', 'blk', 'sub', 'rep')), parts along dimension 0, may hold values from -6 to 6
- expert_ids: int32 [4096, 8], P(('dom', 'blk', 'sub', 'rep')), parts along dimension 0, may hold values from 0 to 127, as said below
- gate_weights: float32 [4096, 8], P(('dom', 'blk', 'sub', 'rep')), parts along dimension 0, may hold values from 0.2 to 2
- w_gate: bfloat16 [2, 768, 2048], P('sub', 'rep', 'blk'), may hold values from -0.125 to 0.125
- w_up: bfloat16 [2, 768, 2048], P('sub', 'rep', 'blk'), may hold values from -0.125 to 0.125
- w_down: bfloat16 [2, 768, 2048], P('sub', 'rep', 'blk'), may hold values from -0.21875 to 0.21875
- cotangent: bfloat16 [4096, 2048], P(('dom', 'blk', 'sub', 'rep')), parts along dimension 0, may hold values from -6 to 6
Outputs:
- mixed: bfloat16 [4096, 2048], P(('dom', 'blk', 'sub', 'rep')), parts along dimension 0
- token_grad: bfloat16 [4096, 2048], P(('dom', 'blk', 'sub', 'rep')), parts along dimension 0
- gate_grad: float32 [4096, 8], P(('dom', 'blk', 'sub', 'rep')), parts along dimension 0
- grad_gate: float32 [4, 768, 2048], P(('dom', 'sub'), 'rep', 'blk'), parts along dimension 0
- grad_up: float32 [4, 768, 2048], P(('dom', 'sub'), 'rep', 'blk'), parts along dimension 0
- grad_down: float32 [4, 768, 2048], P(('dom', 'sub'), 'rep', 'blk'), parts along dimension 0
There are 2 independent parts, one for each index of `dom`. A program takes and returns all parts, laid end to end along the dimension named above; an argument that names none is the same for every part. Nothing has to cross between parts.
Inputs may be any that keep to these rules, and one draw needn't show every extreme that they name: `expert_ids`: each row names 8 different experts. Among the 128 rows of one device, each expert below 2 is named by 1 to 12 rows, and in every draw some expert below 2 is named by 12 rows on every device of one blk index.
All inputs are finite; a program needn't handle non-finite values.
Results may differ from a plain program's by a relative error of at most 0.02.
Values may be sent and summed in bfloat16 or wider, within the bound.
A program may use at most 64 MiB of HBM per device.

v0:
```python
import jax
import jax.numpy as jnp
from jax import lax
from jax.sharding import PartitionSpec as P

NUM_EXPERTS = 128
TOPK = 8
CAP = 12


def silu_pair(pre_act):
    sigmoid_v = jax.nn.sigmoid(pre_act)
    return (pre_act * sigmoid_v, sigmoid_v * (1.0 + pre_act * (1.0 - sigmoid_v)))


def on_device(tokens, expert_ids, gate_weights, w_gate, w_up, w_down, cotangent):
    tok_count = tokens.shape[0]
    local_experts = w_gate.shape[0]
    n_window = local_experts * lax.axis_size("sub")
    capacity = CAP
    total_tokens = tok_count * lax.axis_size("blk") * lax.axis_size("sub") * lax.axis_size("rep")
    grad_scale = (total_tokens * TOPK / NUM_EXPERTS) ** (-0.5)
    zero_low = jnp.zeros((), jnp.bfloat16)
    expert_iota = lax.iota(jnp.int32, n_window)
    named_hits = expert_ids[:, :, None] == expert_iota[None, None, :]
    picked = jnp.sum(named_hits.astype(jnp.int32), axis=1)
    weight_of = jnp.sum(jnp.where(named_hits, gate_weights[:, :, None], 0.0), axis=1)
    before = jnp.cumsum(picked, axis=0) - picked
    slot_iota = lax.iota(jnp.int32, capacity)
    placed = (before[None, :, :] == slot_iota[:, None, None]) & (picked[None, :, :] > 0)
    row_iota = lax.iota(jnp.int32, tok_count)
    slot_row = jnp.sum(jnp.where(placed, row_iota[None, :, None], 0), axis=1)
    slot_live = jnp.any(placed, axis=1)
    slot_gate = jnp.sum(jnp.where(placed, weight_of[None, :, :], 0.0), axis=1)
    slot_tokens = jnp.where(slot_live[:, :, None], tokens[slot_row], zero_low)
    slot_cotan = jnp.where(slot_live[:, :, None], cotangent[slot_row], zero_low)
    slot_dout = (slot_cotan.astype(jnp.float32) * slot_gate[:, :, None]).astype(jnp.bfloat16)
    rows_mine, dout_mine = (
        lax.all_to_all(slot_tokens, "sub", split_axis=1, concat_axis=0, tiled=True),
        lax.all_to_all(slot_dout, "sub", split_axis=1, concat_axis=0, tiled=True),
    )
    rows_all, dout_all = (
        lax.all_gather(rows_mine, "rep", axis=0, tiled=True),
        lax.all_gather(dout_mine, "rep", axis=0, tiled=True),
    )
    full_gate, full_up, full_down = (
        lax.all_gather(w_gate, "blk", axis=2, tiled=True),
        lax.all_gather(w_up, "blk", axis=2, tiled=True),
        lax.all_gather(w_down, "blk", axis=2, tiled=True),
    )
    pre_gate = jnp.einsum("red,efd->ref", rows_all, full_gate, preferred_element_type=jnp.float32)
    pre_up = jnp.einsum("red,efd->ref", rows_all, full_up, preferred_element_type=jnp.float32)
    activated, silu_slope = silu_pair(pre_gate)
    hidden = (activated * pre_up).astype(jnp.bfloat16)
    out_sum = lax.psum_scatter(
        jnp.einsum("ref,efd->red", hidden, full_down, preferred_element_type=jnp.float32).astype(
            jnp.bfloat16
        ),
        "rep",
        scatter_dimension=0,
        tiled=True,
    )
    slot_out = lax.all_to_all(out_sum, "sub", split_axis=0, concat_axis=1, tiled=True)
    down_term = (
        jnp.einsum("ref,red->efd", hidden, dout_all, preferred_element_type=jnp.float32)
        * grad_scale
    ).astype(jnp.bfloat16)
    down_back = lax.all_to_all(down_term[None], "blk", split_axis=3, concat_axis=0, tiled=True)
    down_owned = jnp.sum(down_back.astype(jnp.float32), axis=0)
    placed_low = placed.astype(jnp.bfloat16)
    mixed_acc = jnp.zeros((tok_count, tokens.shape[1]), jnp.float32)
    for expert in range(n_window):
        picked_rows = jnp.einsum(
            "ct,cd->td",
            placed_low[:, :, expert],
            slot_out[:, expert],
            preferred_element_type=jnp.float32,
        )
        mixed_acc = mixed_acc + weight_of[:, expert : expert + 1] * picked_rows
    mixed = mixed_acc.astype(jnp.bfloat16)
    slot_dot = jnp.sum(slot_cotan.astype(jnp.float32) * slot_out.astype(jnp.float32), axis=2)
    token_dot = jnp.sum(jnp.where(placed, slot_dot[:, None, :], 0.0), axis=0)
    gate_grad = jnp.sum(jnp.where(named_hits, token_dot[:, None, :], 0.0), axis=2)
    dhidden = jnp.einsum("red,efd->ref", dout_all, full_down, preferred_element_type=jnp.float32)
    dpre_gate = (dhidden * pre_up * silu_slope).astype(jnp.bfloat16)
    dpre_up = (dhidden * activated).astype(jnp.bfloat16)
    first = jnp.einsum("ref,efd->red", dpre_gate, full_gate, preferred_element_type=jnp.float32)
    in_sum = lax.psum_scatter(
        (
            first + jnp.einsum("ref,efd->red", dpre_up, full_up, preferred_element_type=jnp.float32)
        ).astype(jnp.bfloat16),
        "rep",
        scatter_dimension=0,
        tiled=True,
    )
    slot_in = lax.all_to_all(in_sum, "sub", split_axis=0, concat_axis=1, tiled=True)
    token_grad = jnp.einsum(
        "cte,ced->td", placed_low, slot_in, preferred_element_type=jnp.float32
    ).astype(jnp.bfloat16)
    both_pre = jnp.stack([dpre_gate, dpre_up])
    proj_term = (
        jnp.einsum("gref,red->gefd", both_pre, rows_all, preferred_element_type=jnp.float32)
        * grad_scale
    ).astype(jnp.bfloat16)
    proj_back = lax.all_to_all(proj_term[None], "blk", split_axis=4, concat_axis=0, tiled=True)
    proj_owned = jnp.sum(proj_back.astype(jnp.float32), axis=0)
    grad_gate = proj_owned[0]
    grad_up = proj_owned[1]
    return (mixed, token_grad, gate_grad, grad_gate, grad_up, down_owned)


def solution(mesh):
    in_specs = (
        P(("dom", "blk", "sub", "rep"), None),
        P(("dom", "blk", "sub", "rep"), None),
        P(("dom", "blk", "sub", "rep"), None),
        P("sub", "rep", "blk"),
        P("sub", "rep", "blk"),
        P("sub", "rep", "blk"),
        P(("dom", "blk", "sub", "rep"), None),
    )
    out_specs = (
        P(("dom", "blk", "sub", "rep"), None),
        P(("dom", "blk", "sub", "rep"), None),
        P(("dom", "blk", "sub", "rep"), None),
        P(("dom", "sub"), "rep", "blk"),
        P(("dom", "sub"), "rep", "blk"),
        P(("dom", "sub"), "rep", "blk"),
    )
    return jax.shard_map(
        on_device, mesh=mesh, in_specs=in_specs, out_specs=out_specs, check_vma=False
    )
```

profile of v0, /device:TPU:0, one launch (start us, length us, event | category | flops | bytes accessed | tf_op | source)
XLA Modules:
  0.0 349.2 jit_solution(12591786999858448248)
XLA Ops:
  11.8 8.5 %all_to_all.90 = bf16[12,2,2048]{2,0,1:T(8,128)(2,1)S(1)} all-to-all(bf16[12,2,2048]{2,0,1:T(8,128)(2,1)S(1)} %copy_select_fusion.1), channel_id=1, replica_groups=mesh['dom'=2,'blk'=4,'sub'=2,'rep'=2] {'sub'}, dimensions={1} | all-to-all | bytes 196608 | tf_op jit(solution)/shard_map/all_to_all | solution.py:39
  20.3 1.9 all_gather.15
  22.2 27.2 %all-gather.6.cloned.1.call-done = bf16[1,384,2048]{2,1,0:T(8,128)(2,1)} async-done(((bf16[1,384,512]{2,1,0:T(8,128)(2,1)}), bf16[1,384,2048]{2,1,0:T(8,128)(2,1)}) %all-gather.6.cloned.1.call-update) | async-done | bytes 1572880 | tf_op jit(solution)/shard_map/all_gather | solution.py:48
  49.4 2.0 fusion.21
  51.4 35.6 %all-gather.4.cloned.1.call-done = bf16[1,384,2048]{2,1,0:T(8,128)(2,1)} async-done(((bf16[1,384,512]{2,1,0:T(8,128)(2,1)}), bf16[1,384,2048]{2,1,0:T(8,128)(2,1)}) %all-gather.4.cloned.1.call-update) | async-done | bytes 1572880 | tf_op jit(solution)/shard_map/all_gather | solution.py:47
  87.0 2.0 fusion.18
  89.0 35.5 %all-gather.8.cloned.1.call-done = bf16[1,384,2048]{2,1,0:T(8,128)(2,1)} async-done(((bf16[1,384,512]{2,1,0:T(8,128)(2,1)}), bf16[1,384,2048]{2,1,0:T(8,128)(2,1)}) %all-gather.8.cloned.1.call-update) | async-done | bytes 1572880 | tf_op jit(solution)/shard_map/all_gather | solution.py:49
  124.5 2.5 fusion.6
  127.0 6.6 %reduce-scatter.3.cloned.1.call-done = bf16[24,1,2048]{2,0,1:T(8,128)(2,1)} async-done(((bf16[48,1,2048]{2,0,1:T(8,128)(2,1)}), bf16[24,1,2048]{2,0,1:T(8,128)(2,1)}) %reduce-scatter.3.cloned.1.call-update) | async-done | bytes 98320 | tf_op jit(solution)/shard_map/reduce_scatter | solution.py:55
  134.2 1.6 reduce.10
  136.5 3.3 all-to-all-start.1
  140.6 3.5 %all-to-all-done.1 = bf16[2,2,12288]{2,1,0:T(2,128)(2,1)S(1)} async-done(((bf16[2,2,12288]{2,1,0:T(2,128)(2,1)}), bf16[2,2,12288]{2,1,0:T(2,128)(2,1)S(1)}, u32[]{:S(2)}, u32[]{:S(2)}) %all-to-all-start.1) | async-done | bytes 98336 | tf_op jit(solution)/shard_map/all_to_all | solution.py:63
  145.9 6.8 %all_to_all.91 = bf16[12,2,2048]{2,0,1:T(8,128)(2,1)S(1)} all-to-all(bf16[12,2,2048]{2,0,1:T(8,128)(2,1)S(1)} %fusion.27), channel_id=1, replica_groups=mesh['dom'=2,'blk'=4,'sub'=2,'rep'=2] {'sub'}, dimensions={1} | all-to-all | bytes 196608 | tf_op jit(solution)/shard_map/all_to_all | solution.py:40
  152.8 1.9 all_gather.19
  154.7 2.1 multiply_convert_fusion.2
  158.3 8.0 %reduce-scatter.5.cloned.1.call-done = bf16[24,1,2048]{2,0,1:T(8,128)(2,1)} async-done(((bf16[48,1,2048]{2,0,1:T(8,128)(2,1)}), bf16[24,1,2048]{2,0,1:T(8,128)(2,1)}) %reduce-scatter.5.cloned.1.call-update) | async-done | bytes 98320 | tf_op jit(solution)/shard_map/reduce_scatter | solution.py:88
  166.3 1.6 reduce.11
  168.6 3.3 all-to-all-start.3
  172.6 5.6 %copy.68 = bf16[1,1,384,2048]{2,1,0,3:T(2,128)(2,1)} copy(bf16[1,1,384,2048]{3,2,1,0:T(8,128)(2,1)S(1)} %fusion.1) | data formatting | bytes 3145728 | tf_op jit(solution)/shard_map/broadcast_in_dim | solution.py:68
  178.2 34.3 %reduce.12 = bf16[2048,384]{1,0:T(8,128)(2,1)S(1)} reduce(bf16[2048,1,1,384]{3,2,1,0:T(2,128)(2,1)} %bitcast.140, bf16[]{:T(256)} %broadcast.59), dimensions={1,2}, to_apply=%bitcast.132.reduce_sub_computation | reduce | bytes 3145730
  212.5 1.9 reshape.169
  214.4 4.8 %all-to-all-start.5 = ((bf16[4,2,98304]{2,1,0:T(2,128)(2,1)}), bf16[4,2,98304]{2,1,0:T(2,128)(2,1)S(1)}, u32[]{:S(2)}, u32[]{:S(2)}) async-start(bf16[4,2,98304]{2,1,0:T(2,128)(2,1)} %reshape.169), calls=%async_computation.7 | async-start | bytes 3145728 | tf_op jit(solution)/shard_map/all_to_all | solution.py:68
  220.3 28.4 %copy.66 = bf16[1,2,1,384,2048]{3,1,2,0,4:T(2,128)(2,1)} copy(bf16[1,2,1,384,2048]{3,4,1,2,0:T(8,128)(2,1)S(1)} %fusion) | data formatting | bytes 6291456 | tf_op jit(solution)/shard_map/broadcast_in_dim | solution.py:105
  248.7 8.0 %all-to-all-done.5 = bf16[4,2,98304]{2,1,0:T(2,128)(2,1)S(1)} async-done(((bf16[4,2,98304]{2,1,0:T(2,128)(2,1)}), bf16[4,2,98304]{2,1,0:T(2,128)(2,1)S(1)}, u32[]{:S(2)}, u32[]{:S(2)}) %all-to-all-start.5) | async-done | bytes 1572896 | tf_op jit(solution)/shard_map/all_to_all | solution.py:68
  256.7 4.9 %all-to-all-start.4 = ((bf16[1,2,1,384,2048]{3,1,2,0,4:T(2,128)(2,1)}), bf16[1,2,1,384,2048]{3,1,2,0,4:T(2,128)(2,1)}, u32[]{:S(2)}, u32[]{:S(2)}) async-start(bf16[1,2,1,384,2048]{3,1,2,0,4:T(2,128)(2,1)} %copy.66), calls=%async_computation.6 | async-start | bytes 6291456 | tf_op jit(solution)/shard_map/all_to_all | solution.py:105
  264.9 2.9 reshape.170
  267.8 3.7 %copy.74 = f32[1,1,384,2048]{2,3,0,1:T(8,128)} copy(bf16[1,1,384,2048]{2,1,0,3:T(2,128)(2,1)} %bitcast.142) | data formatting | bytes 4718592
  271.5 2.1 reduce_sum.94
  274.8 56.9 %all-to-all-done.4 = bf16[1,2,1,384,2048]{3,1,2,0,4:T(2,128)(2,1)} async-done(((bf16[1,2,1,384,2048]{3,1,2,0,4:T(2,128)(2,1)}), bf16[1,2,1,384,2048]{3,1,2,0,4:T(2,128)(2,1)}, u32[]{:S(2)}, u32[]{:S(2)}) %all-to-all-start.4) | async-done | bytes 3145760 | tf_op jit(solution)/shard_map/all_to_all | solution.py:105
  331.7 5.7 %convert_reduce_fusion = f32[2,384,512]{1,0,2:T(2,128)S(1)} fusion(bf16[2,384,4,512]{1,0,3,2:T(2,128)(2,1)} %bitcast.65), kind=kLoop, calls=%fused_computation.2 | loop fusion | flops 2752512 | bytes 4718592 | tf_op jit(solution)/shard_map/reduce_sum | solution.py:106
  338.6 2.1 copy.70
  340.7 2.0 copy.69
  (67 shorter events, 17.9 us)
Async XLA Ops:
  7.2 3.7 %copy-start = (bf16[128,2048]{1,0:T(8,128)(2,1)S(1)}, bf16[128,2048]{1,0:T(8,128)(2,1)}, u32[]{:S(2)}) copy-start(bf16[128,2048]{1,0:T(8,128)(2,1)} %param.7) | copy-start | bytes 1572868
  7.2 42.2 %all-gather.6.cloned.1.call-start = ((), (), s32[]{:S(2)}) async-start(), calls=%async_computation.9 | async-start | bytes 1966080 | tf_op jit(solution)/shard_map/all_gather | solution.py:48
  7.9 79.1 %all-gather.4.cloned.1.call-start = ((), (), s32[]{:S(2)}) async-start(), calls=%async_computation.8 | async-start | bytes 1966080 | tf_op jit(solution)/shard_map/all_gather | solution.py:47
  8.7 115.9 %all-gather.8.cloned.1.call-start = ((), (), s32[]{:S(2)}) async-start(), calls=%async_computation.10 | async-start | bytes 1966080 | tf_op jit(solution)/shard_map/all_gather | solution.py:49
  9.4 124.2 %reduce-scatter.3.cloned.1.call-start = ((), (), s32[]{:S(2)}) async-start(), calls=%async_computation.11 | async-start | bytes 294912 | tf_op jit(solution)/shard_map/reduce_scatter | solution.py:55
  89.0 50.9 %copy-start.3 = (bf16[128,2048]{1,0:T(8,128)(2,1)S(1)}, bf16[128,2048]{1,0:T(8,128)(2,1)}, u32[]{:S(2)}) copy-start(bf16[128,2048]{1,0:T(8,128)(2,1)} %param.13) | copy-start | bytes 1572868
  127.0 18.1 %copy-start.4 = (s32[128,8]{0,1:T(8,128)S(1)}, s32[128,8]{0,1:T(8,128)}, u32[]{:S(2)}) copy-start(s32[128,8]{0,1:T(8,128)} %param.8) | copy-start | bytes 12292
  127.0 18.1 %copy-start.5 = (f32[128,8]{0,1:T(8,128)S(1)}, f32[128,8]{0,1:T(8,128)}, u32[]{:S(2)}) copy-start(f32[128,8]{0,1:T(8,128)} %param.9) | copy-start | bytes 12292
  136.5 7.6 %all-to-all-start.1 = ((bf16[2,2,12288]{2,1,0:T(2,128)(2,1)}), bf16[2,2,12288]{2,1,0:T(2,128)(2,1)S(1)}, u32[]{:S(2)}, u32[]{:S(2)}) async-start(bf16[2,2,12288]{2,1,0:T(2,128)(2,1)} %reshape.167), calls=%async_computation.2 | async-start | bytes 196608 | tf_op jit(solution)/shard_map/all_to_all | solution.py:63
  139.8 26.5 %reduce-scatter.5.cloned.1.call-start = ((), (), s32[]{:S(2)}) async-start(), calls=%async_computation.12 | async-start | bytes 294912 | tf_op jit(solution)/shard_map/reduce_scatter | solution.py:88
  145.0 11.9 %copy-start.2 = (bf16[1,384,2048]{2,1,0:T(8,128)(2,1)S(1)}, bf16[1,384,2048]{2,1,0:T(8,128)(2,1)}, u32[]{:S(2)}) copy-start(bf16[1,384,2048]{2,1,0:T(8,128)(2,1)} %all-gather.4.cloned.1.call-done) | copy-start | bytes 4718596
  154.7 2.5 copy-start.1
  168.6 45.7 %all-to-all-start.3 = ((bf16[2,2,12288]{2,1,0:T(2,128)(2,1)}), bf16[2,2,12288]{2,1,0:T(2,128)(2,1)S(1)}, u32[]{:S(2)}, u32[]{:S(2)}) async-start(bf16[2,2,12288]{2,1,0:T(2,128)(2,1)} %reshape.171), calls=%async_computation.5 | async-start | bytes 196608 | tf_op jit(solution)/shard_map/all_to_all | solution.py:96
  214.4 42.3 %all-to-all-start.5 = ((bf16[4,2,98304]{2,1,0:T(2,128)(2,1)}), bf16[4,2,98304]{2,1,0:T(2,128)(2,1)S(1)}, u32[]{:S(2)}, u32[]{:S(2)}) async-start(bf16[4,2,98304]{2,1,0:T(2,128)(2,1)} %reshape.169), calls=%async_computation.7 | async-start | bytes 3145728 | tf_op jit(solution)/shard_map/all_to_all | solution.py:68
  256.7 75.0 %all-to-all-start.4 = ((bf16[1,2,1,384,2048]{3,1,2,0,4:T(2,128)(2,1)}), bf16[1,2,1,384,2048]{3,1,2,0,4:T(2,128)(2,1)}, u32[]{:S(2)}, u32[]{:S(2)}) async-start(bf16[1,2,1,384,2048]{3,1,2,0,4:T(2,128)(2,1)} %copy.66), calls=%async_computation.6 | async-start | bytes 6291456 | tf_op jit(solution)/shard_map/all_to_all | solution.py:105
Sparse Core Ops, SparseCore 0:
  9.6 39.7 all-gather.5
  51.0 35.9 all-gather.3
  88.5 35.9 all-gather.7
  127.2 6.4 reduce-scatter.2
  158.5 7.8 reduce-scatter.4
where the time goes:
time: 350 us; the launch traced here: 349 us
  waiting for transfers between devices  183 us (52%)
  local copies, waits for them, and re-layouts  53.1 us (15%)
  other arithmetic  48.7 us (14%)
  blocking collectives  19.2 us (5%)
  starting transfers between devices  16.6 us (5%)
  matrix products  14.3 us (4%)
  between operations  14.1 us (4%)
    all_to_all x1, waiting for transfers between devices, on_device(): lax.all_to_all(proj_term[None], 'blk', split_axis=4, concat_axis=0, tiled...  56.9 us
    all_gather x1, waiting for transfers between devices, on_device(): lax.all_gather(w_gate, 'blk', axis=2, tiled=True)  35.6 us
    all_gather x1, waiting for transfers between devices, on_device(): lax.all_gather(w_down, 'blk', axis=2, tiled=True)  35.5 us
    unnamed x1, other arithmetic  34.3 us
    broadcast_in_dim x1, local copies, waits for them, and re-layouts, on_device(): proj_term[None]  28.4 us
    all_gather x1, waiting for transfers between devices, on_device(): lax.all_gather(w_up, 'blk', axis=2, tiled=True)  27.2 us
    unnamed x22, local copies, waits for them, and re-layouts  15.4 us
    all_to_all x1, blocking collectives, on_device(): lax.all_to_all(slot_tokens, 'sub', split_axis=1, concat_axis=0, tiled=True)  8.48 us
  transfers between devices with their start and end apart: 9, of which 8 were waited for; matrix products, arithmetic and copies ran while one was open for 26% of the time, Pallas kernels for 0%

commit v1 on v0

v1 whole, which is shorter than its diff:
```python
import functools

import jax
import jax.numpy as jnp
from jax import lax
from jax.experimental import pallas as pl
from jax.experimental.pallas import tpu as pltpu
from jax.sharding import PartitionSpec as P

NUM_EXPERTS = 128
TOPK = 8
CAP = 12
MESH = pl.DeviceIdType.MESH
BF16 = jnp.bfloat16
F32 = jnp.float32


def each(low, high, body):
    if high - low <= 8:
        for i in range(low, high):
            body(i)
    else:

        def step(i, carry):
            body(i)
            return carry

        lax.fori_loop(low, high, step, 0)


def div_mod(k, n):
    if isinstance(k, int):
        return k // n, k % n
    return lax.div(k, n), lax.rem(k, n)


def steps_of(v, width, count):
    out = jnp.zeros_like(v)
    for m in range(1, count):
        out = out + (v >= m * width).astype(jnp.int32)
    return out


def dot(a, b):
    return jnp.dot(a, b, preferred_element_type=F32)


def dot_nt(a, b):
    return lax.dot_general(a, b, (((1,), (1,)), ((), ())), preferred_element_type=F32)


def dot_tn(a, b):
    return lax.dot_general(a, b, (((0,), (0,)), ((), ())), preferred_element_type=F32)


def as_mask(cond):
    return jnp.where(cond, 1.0, 0.0).astype(BF16)


def kernel(
    dims,
    ids_ref,
    gw_ref,
    tok_ref,
    cot_ref,
    wg_ref,
    wu_ref,
    wd_ref,
    mixed_ref,
    tgrad_ref,
    ggrad_ref,
    gg_ref,
    gu_ref,
    gd_ref,
    mt_ref,
    wt_ref,
    send1,
    recv1,
    cots,
    xs,
    dos,
    part_own,
    part_send,
    part_recv,
    hid,
    px_own,
    px_send,
    px_recv,
    fin,
    back,
    disp_s,
    disp_r,
    fwd_s,
    fwd_r,
    rs_s,
    rs_r,
    ag_s,
    ag_r,
    px_s,
    px_r,
    bk_s,
    bk_r,
):
    n_blk, n_sub, n_rep, halves, pack, scale = dims
    tok_count = tok_ref.shape[0]
    d_blk = wg_ref.shape[2]
    ff = wg_ref.shape[1]
    width = d_blk // halves
    per_blk = n_sub * n_rep
    chunk = per_blk * CAP
    rows = n_sub * pack
    lanes = mt_ref.shape[1]
    kinds = 2 * halves
    b = lax.axis_index("blk")
    s = lax.axis_index("sub")
    r = lax.axis_index("rep")
    other = 1 - r

    def wrap(v, n):
        return lax.rem(v + n, n)

    barrier = pltpu.get_barrier_semaphore()
    group = n_blk * n_sub * n_rep

    def greet(k):
        db, rest = div_mod(k, n_sub * n_rep)
        ds, dr = div_mod(rest, n_rep)
        pl.semaphore_signal(
            barrier,
            inc=1,
            device_id={"blk": wrap(b + db, n_blk), "sub": wrap(s + ds, n_sub), "rep": wrap(r + dr, n_rep)},
            device_id_type=MESH,
        )

    each(1, group, greet)

    lane = lax.broadcasted_iota(jnp.int32, (tok_count, lanes), 1)
    lane_exp = steps_of(lane, pack, n_sub)
    lane_in = lane - lane_exp * pack
    lane_kind = steps_of(lane_in, CAP, kinds + 1)
    lane_slot = lane_in - lane_kind * CAP
    picked = jnp.zeros((tok_count, lanes), F32)
    weight = jnp.zeros((tok_count, lanes), F32)
    for k in range(ids_ref.shape[1]):
        hit = ids_ref[:, k : k + 1] == lane_exp
        picked = picked + jnp.where(hit, 1.0, 0.0)
        weight = weight + jnp.where(hit, gw_ref[:, k : k + 1], 0.0)
    row_i = lax.broadcasted_iota(jnp.int32, (tok_count, tok_count), 0)
    col_i = lax.broadcasted_iota(jnp.int32, (tok_count, tok_count), 1)
    before = dot(as_mask(col_i < row_i), picked.astype(BF16))
    live = (lane_kind < kinds) & (lane < rows)
    placed = (before == lane_slot.astype(F32)) & (picked > 0.0) & live
    mt = jnp.where(placed, 1.0, 0.0)
    wt = jnp.where(placed, weight, 0.0)
    mt_ref[...] = mt
    wt_ref[...] = wt
    sel = mt.T[:rows]
    slot_gate = jnp.sum(wt.T[:rows], axis=1, keepdims=True)
    sub_i = lax.broadcasted_iota(jnp.int32, (rows, 1), 0)
    sub_exp = steps_of(sub_i, pack, n_sub)
    sub_kind = steps_of(sub_i - sub_exp * pack, CAP, kinds + 1)
    is_cot = sub_kind == 1
    for h in range(1, halves):
        is_cot = is_cot | (sub_kind == 2 * h + 1)
    row_scale = jnp.where(is_cot, slot_gate, 1.0)
    takes = [jnp.where(sub_kind == x, sel, 0.0).astype(BF16) for x in range(kinds)]

    def columns(blk, h):
        return pl.ds(pl.multiple_of(blk * d_blk + h * width, width), width)

    my_q = b * per_blk + r * n_sub + s

    def disp_copy(k):
        db, ds = div_mod(k, n_sub)
        dst_b, dst_s = wrap(b + db, n_blk), wrap(s + ds, n_sub)
        return pltpu.make_async_remote_copy(
            src_ref=send1.at[dst_b, dst_s],
            dst_ref=recv1.at[my_q],
            send_sem=disp_s.at[k],
            recv_sem=disp_r.at[k],
            device_id={"blk": dst_b, "sub": dst_s},
            device_id_type=MESH,
        )

    def fwd_copy(k):
        db, ds = div_mod(k, n_sub)
        q = wrap(b - db, n_blk) * per_blk + r * n_sub + wrap(s - ds, n_sub)
        return pltpu.make_async_remote_copy(
            src_ref=recv1.at[q],
            dst_ref=recv1.at[q],
            send_sem=fwd_s.at[k],
            recv_sem=fwd_r.at[k],
            device_id={"rep": other},
            device_id_type=MESH,
        )

    def gather(db):
        blk = wrap(b + db, n_blk)
        acc = None
        for h in range(halves):
            cols = columns(blk, h)
            term = dot(takes[2 * h], tok_ref[:, cols]) + dot(takes[2 * h + 1], cot_ref[:, cols])
            acc = term if acc is None else acc + term
        send1[blk] = (acc * row_scale).astype(BF16).reshape(n_sub, pack, width)

    def send_rows(db):
        each(0, n_sub, lambda ds: disp_copy(db * n_sub + ds).start())

    gather(1)
    pl.semaphore_wait(barrier, group - 1)
    send_rows(1)

    def gather_send(db):
        gather(db)
        send_rows(db)

    each(2, n_blk, gather_send)
    gather(0)
    each(1, n_sub, lambda ds: disp_copy(ds).start())
    recv1[my_q] = send1[b, s]
    fwd_copy(0).start()

    def forward(db):
        def one(ds):
            k = db * n_sub + ds
            disp_copy(k).wait_recv()
            fwd_copy(k).start()

        each(0, n_sub, one)

    def forward_first(ds):
        disp_copy(ds).wait_recv()
        fwd_copy(ds).start()

    each(1, n_sub, forward_first)

    prow = lax.broadcasted_iota(jnp.int32, (chunk, per_blk * pack), 0)
    pcol = lax.broadcasted_iota(jnp.int32, (chunk, per_blk * pack), 1)
    prow_g = steps_of(prow, CAP, per_blk)
    pcol_g = steps_of(pcol, pack, per_blk)
    prow_c = prow - prow_g * CAP
    pcol_j = pcol - pcol_g * pack
    unpack = [as_mask((prow_g == pcol_g) & (pcol_j == x * CAP + prow_c)) for x in range(kinds)]

    def cot_rows(db):
        blk = wrap(b + db, n_blk)
        acc = None
        for h in range(halves):
            term = dot(takes[2 * h], cot_ref[:, columns(blk, h)])
            acc = term if acc is None else acc + term
        cots[blk] = acc.astype(BF16)

    each(0, n_blk, cot_rows)

    def rs_copy(db):
        return pltpu.make_async_remote_copy(
            src_ref=part_send.at[db],
            dst_ref=part_recv.at[db],
            send_sem=rs_s.at[db],
            recv_sem=rs_r.at[db],
            device_id={"blk": wrap(b - db, n_blk)},
            device_id_type=MESH,
        )

    def partial(db):
        blk = wrap(b - db, n_blk)
        each(0, n_sub, lambda ds: fwd_copy(db * n_sub + ds).wait_recv())
        block = recv1[pl.ds(blk * per_blk, per_blk)].reshape(per_blk * pack, width)
        for h in range(halves):
            xs[blk, :, h * width : (h + 1) * width] = dot(unpack[2 * h], block).astype(BF16)
            dos[blk, :, h * width : (h + 1) * width] = dot(unpack[2 * h + 1], block).astype(BF16)
        x, do = xs[blk], dos[blk]
        return dot_nt(x, wg_ref[0]), dot_nt(x, wu_ref[0]), dot_nt(do, wd_ref[0])

    def partial_send(db):
        for m, value in enumerate(partial(db)):
            part_send[db, :, m * ff : (m + 1) * ff] = value.astype(BF16)
        rs_copy(db).start()

    forward(1)
    for m, value in enumerate(partial(0)):
        part_own[:, m * ff : (m + 1) * ff] = value

    def middle(db):
        forward(db + 1)
        partial_send(db)

    each(1, n_blk - 1, middle)
    partial_send(n_blk - 1)

    def add_part(db):
        rs_copy(db).wait_recv()
        part_own[...] += part_recv[db].astype(F32)

    each(1, n_blk, add_part)
    pre_gate = part_own[:, :ff]
    pre_up = part_own[:, ff : 2 * ff]
    dhid = part_own[:, 2 * ff :]
    sig = jax.nn.sigmoid(pre_gate)
    act = pre_gate * sig
    slope = sig * (1.0 + pre_gate * (1.0 - sig))
    hid[b, :, :ff] = (act * pre_up).astype(BF16)
    hid[b, :, ff : 2 * ff] = (dhid * pre_up * slope).astype(BF16)
    hid[b, :, 2 * ff :] = (dhid * act).astype(BF16)

    def ag_copy(db):
        return pltpu.make_async_remote_copy(
            src_ref=hid.at[b],
            dst_ref=hid.at[b],
            send_sem=ag_s.at[db],
            recv_sem=ag_r.at[db],
            device_id={"blk": wrap(b + db, n_blk)},
            device_id_type=MESH,
        )

    each(1, n_blk, lambda db: ag_copy(db).start())

    srow = lax.broadcasted_iota(jnp.int32, (rows, chunk), 0)
    scol = lax.broadcasted_iota(jnp.int32, (rows, chunk), 1)
    srow_s = steps_of(srow, pack, n_sub)
    srow_j = srow - srow_s * pack
    srow_x = steps_of(srow_j, CAP, kinds + 1)
    srow_at = srow_s * CAP + srow_j - srow_x * CAP

    def repack(rep):
        at = scol == srow_at + rep * (n_sub * CAP)
        return [as_mask(at & (srow_x == x)) for x in range(kinds)]

    to_mine, to_other = repack(r), repack(other)

    def px_copy(db):
        return pltpu.make_async_remote_copy(
            src_ref=px_send.at[db],
            dst_ref=px_recv.at[db],
            send_sem=px_s.at[db],
            recv_sem=px_r.at[db],
            device_id={"rep": other},
            device_id_type=MESH,
        )

    def bk_copy(k):
        db, ds = div_mod(k, n_sub)
        dst_s = wrap(s + ds, n_sub)
        return pltpu.make_async_remote_copy(
            src_ref=fin.at[db, dst_s],
            dst_ref=back.at[b, s],
            send_sem=bk_s.at[k],
            recv_sem=bk_r.at[k],
            device_id={"blk": wrap(b - db, n_blk), "sub": dst_s},
            device_id_type=MESH,
        )

    def outputs(db):
        blk = wrap(b - db, n_blk)
        out = dot(hid[blk, :, :ff], wd_ref[0]).astype(BF16)
        into = dot(hid[blk, :, ff : 2 * ff], wg_ref[0]) + dot(hid[blk, :, 2 * ff :], wu_ref[0])
        into = into.astype(BF16)

        def packed(masks):
            acc = None
            for h in range(halves):
                cols = slice(h * width, (h + 1) * width)
                term = dot(masks[2 * h], out[:, cols]) + dot(masks[2 * h + 1], into[:, cols])
                acc = term if acc is None else acc + term
            return acc.astype(BF16).reshape(n_sub, pack, width)

        px_send[db] = packed(to_other)
        px_copy(db).start()
        px_own[db] = packed(to_mine)

    def finish(db):
        px_copy(db).wait_recv()
        fin[db] = (px_own[db].astype(F32) + px_recv[db].astype(F32)).astype(BF16)

    outputs(0)

    def rest(db):
        ag_copy(db).wait_recv()
        outputs(db)
        finish(db)
        each(0, n_sub, lambda ds: bk_copy(db * n_sub + ds).start())

    each(1, n_blk, rest)
    finish(0)
    each(1, n_sub, lambda ds: bk_copy(ds).start())
    back[b, s] = fin[0, s]

    x_all = xs[...].reshape(n_blk * chunk, d_blk)
    do_all = dos[...].reshape(n_blk * chunk, d_blk)
    gd_ref[0] = dot_tn(hid[:, :, :ff].reshape(n_blk * chunk, ff), do_all) * scale
    gg_ref[0] = dot_tn(hid[:, :, ff : 2 * ff].reshape(n_blk * chunk, ff), x_all) * scale
    gu_ref[0] = dot_tn(hid[:, :, 2 * ff :].reshape(n_blk * chunk, ff), x_all) * scale

    wt_all = wt_ref[:, :rows]
    wt_high = wt_all.astype(BF16)
    wt_low = (wt_all - wt_high.astype(F32)).astype(BF16)
    mt_low = mt_ref[:, :rows].astype(BF16)
    kind_row = lane_kind[:, :rows]
    none = jnp.zeros((tok_count, rows), BF16)

    def collect(db, dots):
        blk = wrap(b + db, n_blk)
        got = back[blk].reshape(rows, width)
        for h in range(halves):
            cols = columns(blk, h)
            high = jnp.where(kind_row == 2 * h, wt_high, none)
            low = jnp.where(kind_row == 2 * h, wt_low, none)
            ones = jnp.where(kind_row == 2 * h + 1, mt_low, none)
            mixed_ref[:, cols] = (dot(high, got) + dot(low, got)).astype(BF16)
            tgrad_ref[:, cols] = dot(ones, got).astype(BF16)
        return dots + jnp.sum(cots[blk].astype(F32) * got.astype(F32), axis=1, keepdims=True)

    each(1, n_sub, lambda ds: bk_copy(ds).wait_recv())
    dots = collect(0, jnp.zeros((rows, 1), F32))

    def step(db, dots):
        each(0, n_sub, lambda ds: bk_copy(db * n_sub + ds).wait_recv())
        return collect(db, dots)

    if n_blk <= 8:
        for db in range(1, n_blk):
            dots = step(db, dots)
    else:
        dots = lax.fori_loop(1, n_blk, step, dots)
    wide = jnp.broadcast_to(dots, (rows, tok_count))
    if lanes > rows:
        wide = jnp.concatenate([wide, jnp.zeros((lanes - rows, tok_count), F32)], axis=0)
    token_dots = mt_ref[...] * wide.T
    picks = []
    for k in range(ids_ref.shape[1]):
        hit = ids_ref[:, k : k + 1] == lane_exp
        picks.append(jnp.sum(jnp.where(hit, token_dots, 0.0), axis=1, keepdims=True))
    ggrad_ref[...] = jnp.concatenate(picks, axis=1)

    each(1, n_blk * n_sub, lambda k: disp_copy(k).wait_send())
    each(0, n_blk * n_sub, lambda k: fwd_copy(k).wait_send())
    each(1, n_blk, lambda db: rs_copy(db).wait_send())
    each(1, n_blk, lambda db: ag_copy(db).wait_send())
    each(0, n_blk, lambda db: px_copy(db).wait_send())
    each(1, n_blk * n_sub, lambda k: bk_copy(k).wait_send())


def on_device(tokens, expert_ids, gate_weights, w_gate, w_up, w_down, cotangent):
    n_blk, n_sub, n_rep = (lax.axis_size(name) for name in ("blk", "sub", "rep"))
    tok_count, d_model = tokens.shape
    _, ff, d_blk = w_gate.shape
    scale = (tok_count * n_blk * n_sub * n_rep * TOPK / NUM_EXPERTS) ** (-0.5)
    halves = 2 if d_blk % 256 == 0 else 1
    width = d_blk // halves
    pack = -(-2 * halves * CAP // 16) * 16
    rows = n_sub * pack
    lanes = -(-rows // 128) * 128
    chunk = n_sub * n_rep * CAP
    pairs = n_blk * n_sub
    dma = pltpu.SemaphoreType.DMA
    vmem = pl.BlockSpec(memory_space=pltpu.VMEM)
    dims = (n_blk, n_sub, n_rep, halves, pack, scale)
    grad = jax.ShapeDtypeStruct((1, ff, d_blk), F32)
    return pl.pallas_call(
        functools.partial(kernel, dims),
        out_shape=(
            jax.ShapeDtypeStruct((tok_count, d_model), BF16),
            jax.ShapeDtypeStruct((tok_count, d_model), BF16),
            jax.ShapeDtypeStruct(gate_weights.shape, F32),
            grad,
            grad,
            grad,
        ),
        in_specs=[vmem] * 7,
        out_specs=(vmem,) * 6,
        scratch_shapes=[
            pltpu.VMEM((tok_count, lanes), F32),
            pltpu.VMEM((tok_count, lanes), F32),
            pltpu.VMEM((n_blk, n_sub, pack, width), BF16),
            pltpu.VMEM((pairs * n_rep, pack, width), BF16),
            pltpu.VMEM((n_blk, rows, width), BF16),
            pltpu.VMEM((n_blk, chunk, d_blk), BF16),
            pltpu.VMEM((n_blk, chunk, d_blk), BF16),
            pltpu.VMEM((chunk, 3 * ff), F32),
            pltpu.VMEM((n_blk, chunk, 3 * ff), BF16),
            pltpu.VMEM((n_blk, chunk, 3 * ff), BF16),
            pltpu.VMEM((n_blk, chunk, 3 * ff), BF16),
            pltpu.VMEM((n_blk, n_sub, pack, width), BF16),
            pltpu.VMEM((n_blk, n_sub, pack, width), BF16),
            pltpu.VMEM((n_blk, n_sub, pack, width), BF16),
            pltpu.VMEM((n_blk, n_sub, pack, width), BF16),
            pltpu.VMEM((n_blk, n_sub, pack, width), BF16),
            dma((pairs,)),
            dma((pairs,)),
            dma((pairs,)),
            dma((pairs,)),
            dma((n_blk,)),
            dma((n_blk,)),
            dma((n_blk,)),
            dma((n_blk,)),
            dma((n_blk,)),
            dma((n_blk,)),
            dma((pairs,)),
            dma((pairs,)),
        ],
        compiler_params=pltpu.CompilerParams(
            collective_id=0, has_side_effects=True, vmem_limit_bytes=56 * 1024 * 1024
        ),
        cost_estimate=pl.CostEstimate(flops=1 << 30, bytes_accessed=8 << 20, transcendentals=chunk * ff),
    )(expert_ids, gate_weights, tokens, cotangent, w_gate, w_up, w_down)


def solution(mesh):
    rows = P(("dom", "blk", "sub", "rep"), None)
    weights = P("sub", "rep", "blk")
    grads = P(("dom", "sub"), "rep", "blk")
    return jax.shard_map(
        on_device,
        mesh=mesh,
        in_specs=(rows, rows, rows, weights, weights, weights, rows),
        out_specs=(rows, rows, rows, grads, grads, grads),
        check_vma=False,
    )
```

time: 350 us -> 58.7 us (0.17)
  waiting for transfers between devices: 183 us -> 0 us
  other arithmetic: 48.7 us -> 0 us
  Pallas kernels: 0 us -> 47.5 us
  local copies, waits for them, and re-layouts: 53.1 us -> 10.2 us
  blocking collectives: 19.2 us -> 0 us
  starting transfers between devices: 16.6 us -> 0 us
  matrix products: 14.3 us -> 0 us
  between operations: 14.1 us -> 0.66 us
    all_gather x3 -> x0, waiting for transfers between devices: 98.3 us -> none  [the longest x1 35.6 us: on_device(): lax.all_gather(w_gate, 'blk', axis=2, tiled=True)]
    all_to_all x4 -> x0, waiting for transfers between devices: 68.5 us -> none  [the longest x1 56.9 us: on_device(): lax.all_to_all(proj_term[None], 'blk', split_axis=4, concat_axis=0, tiled...]
    pallas_call x0 -> x1, Pallas kernels: none -> 47.5 us  [on_device(): pl.pallas_call(functools.partial(kernel, dims), out_shape=(jax.ShapeDtype...]
    unnamed x1 -> x0, other arithmetic: 34.3 us -> none
    broadcast_in_dim x2 -> x0, local copies, waits for them, and re-layouts: 34 us -> none  [the longest x1 28.4 us: on_device(): proj_term[None]]
    all_to_all x4 -> x0, starting transfers between devices: 16.4 us -> none  [the longest x1 4.86 us: on_device(): lax.all_to_all(proj_term[None], 'blk', split_axis=4, concat_axis=0, tiled...]
    all_to_all x2 -> x0, blocking collectives: 15.3 us -> none  [the longest x1 8.48 us: on_device(): lax.all_to_all(slot_tokens, 'sub', split_axis=1, concat_axis=0, tiled=True)]
    reduce_scatter x2 -> x0, waiting for transfers between devices: 14.6 us -> none  [the longest x1 7.98 us: on_device(): lax.psum_scatter((first + jnp.einsum('ref,efd->red', dpre_up, full_up, pr...]
  transfers between devices with their start and end apart: 9 -> 0, of which waited for: 8 -> 0; matrix products, arithmetic and copies ran while one was open for 26% -> 0% of each run, Pallas kernels for 0% -> 0%
where the time goes in v1:
time: 58.7 us; the launch traced here: 58.4 us
  Pallas kernels  47.5 us (81%)
  local copies, waits for them, and re-layouts  10.2 us (17%)
  between operations  0.66 us (1%)
    pallas_call x1, Pallas kernels, on_device(): pl.pallas_call(functools.partial(kernel, dims), out_shape=(jax.ShapeDtype...  47.5 us
    unnamed x17, local copies, waits for them, and re-layouts  8.62 us
    pallas_call x1, local copies, waits for them, and re-layouts, on_device(): pl.pallas_call(functools.partial(kernel, dims), out_shape=(jax.ShapeDtype...  1.56 us

profile of v1, /device:TPU:0, one launch (start us, length us, event | category | flops | bytes accessed | tf_op | source)
XLA Modules:
  0.0 58.4 jit_solution(17756819752590733245)
XLA Ops:
  0.6 0.0 copy-start.4
  0.6 1.4 %copy.13.ids_ref = s32[128,8]{1,0:T(8,128)} copy(s32[128,8]{0,1:T(8,128)} %param.8) | data formatting | bytes 8192 | tf_op args[1]
  2.1 0.0 copy-done.4
  2.1 0.7 %copy.14.gw_ref = f32[128,8]{1,0:T(8,128)} copy(f32[128,8]{0,1:T(8,128)S(1)} %copy-done.4) | data formatting | bytes 8192 | tf_op args[2]
  2.8 47.5 %shard_map.118 = (bf16[128,2048]{1,0:T(8,128)(2,1)}, bf16[128,2048]{1,0:T(8,128)(2,1)}, f32[128,8]{1,0:T(8,128)}, f32[1,384,512]{2,1,0:T(8,128)}, f32[1,384,512]{2,1,0:T(8,128)}, /*index=5*/f32[1,384,512]{2,1,0:T(8,128)}) custom-call(s32[128,8]{1,0:T(8,128)} %copy.13.ids_ref, f32[128,8]{1,0:T(8,128)} %copy.14.gw_ref, bf16[128,2048]{1,0:T(8,128)(2,1)} %tok_ref.1, ...), custom_call_target="tpu_custom_call" | custom-call | flops 1073741824 | bytes 8388608 | tf_op jit(solution)/shard_map/pallas_call | solution.py:459
  50.3 0.0 copy-start.3
  50.4 1.6 %copy.15 = f32[128,8]{0,1:T(8,128)} copy(f32[128,8]{1,0:T(8,128)} %get-tuple-element.8) | data formatting | bytes 8192 | tf_op jit(solution)/shard_map/pallas_call | solution.py:459
  51.9 0.0 copy-start.2
  51.9 2.0 %copy.21 = bf16[128,2048]{1,0:T(8,128)(2,1)} copy(bf16[128,2048]{1,0:T(8,128)(2,1)} %get-tuple-element.18) | data formatting | bytes 1048576
  53.9 0.0 copy-done.3
  53.9 0.8 %copy.22 = bf16[128,2048]{1,0:T(8,128)(2,1)} copy(bf16[128,2048]{1,0:T(8,128)(2,1)S(1)} %copy-done.3) | data formatting | bytes 1048576
  54.7 0.0 copy-done.2
  54.7 0.0 copy-start.1
  54.7 0.9 %copy.23 = f32[1,384,512]{2,1,0:T(8,128)} copy(f32[1,384,512]{2,1,0:T(8,128)S(1)} %copy-done.2) | data formatting | bytes 1572864
  55.5 0.5 copy-done.1
  56.1 0.0 copy-start
  56.1 0.9 %copy.24 = f32[1,384,512]{2,1,0:T(8,128)} copy(f32[1,384,512]{2,1,0:T(8,128)S(1)} %copy-done.1) | data formatting | bytes 1572864
  57.0 0.5 copy-done
  57.5 0.9 %copy.25 = f32[1,384,512]{2,1,0:T(8,128)} copy(f32[1,384,512]{2,1,0:T(8,128)S(1)} %copy-done) | data formatting | bytes 1572864
Async XLA Ops:
  0.6 1.4 %copy-start.4 = (f32[128,8]{0,1:T(8,128)S(1)}, f32[128,8]{0,1:T(8,128)}, u32[]{:S(2)}) copy-start(f32[128,8]{0,1:T(8,128)} %param.9) | copy-start | bytes 12292
  50.3 3.5 %copy-start.3 = (bf16[128,2048]{1,0:T(8,128)(2,1)S(1)}, bf16[128,2048]{1,0:T(8,128)(2,1)}, u32[]{:S(2)}) copy-start(bf16[128,2048]{1,0:T(8,128)(2,1)} %get-tuple-element.19) | copy-start | bytes 1572868
  51.9 2.8 %copy-start.2 = (f32[1,384,512]{2,1,0:T(8,128)S(1)}, f32[1,384,512]{2,1,0:T(8,128)}, u32[]{:S(2)}) copy-start(f32[1,384,512]{2,1,0:T(8,128)} %get-tuple-element.21) | copy-start | bytes 2359300
  54.7 1.4 %copy-start.1 = (f32[1,384,512]{2,1,0:T(8,128)S(1)}, f32[1,384,512]{2,1,0:T(8,128)}, u32[]{:S(2)}) copy-start(f32[1,384,512]{2,1,0:T(8,128)} %get-tuple-element.22) | copy-start | bytes 2359300
  56.1 1.4 %copy-start = (f32[1,384,512]{2,1,0:T(8,128)S(1)}, f32[1,384,512]{2,1,0:T(8,128)}, u32[]{:S(2)}) copy-start(f32[1,384,512]{2,1,0:T(8,128)} %get-tuple-element.23) | copy-start | bytes 2359300

commit v2 on v1

--- a/solution.py
+++ b/solution.py
@@ -1,4 +1,5 @@
 import functools
+import math
 
 import jax
 import jax.numpy as jnp
@@ -63,31 +64,29 @@
     gw_ref,
     tok_ref,
     cot_ref,
+    wg_hbm,
+    wu_hbm,
+    wd_hbm,
+    sel_ref,
+    selw_ref,
+    cots,
+    xs,
+    dos,
+    hid,
+    back,
     wg_ref,
     wu_ref,
     wd_ref,
-    mixed_ref,
-    tgrad_ref,
-    ggrad_ref,
-    gg_ref,
-    gu_ref,
-    gd_ref,
-    mt_ref,
-    wt_ref,
     send1,
     recv1,
-    cots,
-    xs,
-    dos,
     part_own,
     part_send,
     part_recv,
-    hid,
     px_own,
     px_send,
     px_recv,
     fin,
-    back,
+    w_s,
     disp_s,
     disp_r,
     fwd_s,
@@ -101,7 +100,7 @@
     bk_s,
     bk_r,
 ):
-    n_blk, n_sub, n_rep, halves, pack, scale = dims
+    n_blk, n_sub, n_rep, halves, pack = dims
     tok_count = tok_ref.shape[0]
     d_blk = wg_ref.shape[2]
     ff = wg_ref.shape[1]
@@ -109,7 +108,6 @@
     per_blk = n_sub * n_rep
     chunk = per_blk * CAP
     rows = n_sub * pack
-    lanes = mt_ref.shape[1]
     kinds = 2 * halves
     b = lax.axis_index("blk")
     s = lax.axis_index("sub")
@@ -118,6 +116,13 @@
 
     def wrap(v, n):
         return lax.rem(v + n, n)
+
+    fetches = [
+        pltpu.make_async_copy(src, dst, w_s.at[i])
+        for i, (src, dst) in enumerate(((wg_hbm, wg_ref), (wu_hbm, wu_ref), (wd_hbm, wd_ref)))
+    ]
+    for fetch in fetches:
+        fetch.start()
 
     barrier = pltpu.get_barrier_semaphore()
     group = n_blk * n_sub * n_rep
@@ -134,35 +139,30 @@
 
     each(1, group, greet)
 
-    lane = lax.broadcasted_iota(jnp.int32, (tok_count, lanes), 1)
-    lane_exp = steps_of(lane, pack, n_sub)
-    lane_in = lane - lane_exp * pack
-    lane_kind = steps_of(lane_in, CAP, kinds + 1)
-    lane_slot = lane_in - lane_kind * CAP
-    picked = jnp.zeros((tok_count, lanes), F32)
-    weight = jnp.zeros((tok_count, lanes), F32)
-    for k in range(ids_ref.shape[1]):
-        hit = ids_ref[:, k : k + 1] == lane_exp
+    sub_i = lax.broadcasted_iota(jnp.int32, (rows, tok_count), 0)
+    sub_exp = steps_of(sub_i, pack, n_sub)
+    sub_in = sub_i - sub_exp * pack
+    sub_kind = steps_of(sub_in, CAP, kinds + 1)
+    sub_slot = sub_in - sub_kind * CAP
+    picked = jnp.zeros((rows, tok_count), F32)
+    weight = jnp.zeros((rows, tok_count), F32)
+    for k in range(ids_ref.shape[0]):
+        hit = ids_ref[k : k + 1, :] == sub_exp
         picked = picked + jnp.where(hit, 1.0, 0.0)
-        weight = weight + jnp.where(hit, gw_ref[:, k : k + 1], 0.0)
+        weight = weight + jnp.where(hit, gw_ref[k : k + 1, :], 0.0)
     row_i = lax.broadcasted_iota(jnp.int32, (tok_count, tok_count), 0)
     col_i = lax.broadcasted_iota(jnp.int32, (tok_count, tok_count), 1)
-    before = dot(as_mask(col_i < row_i), picked.astype(BF16))
-    live = (lane_kind < kinds) & (lane < rows)
-    placed = (before == lane_slot.astype(F32)) & (picked > 0.0) & live
-    mt = jnp.where(placed, 1.0, 0.0)
-    wt = jnp.where(placed, weight, 0.0)
-    mt_ref[...] = mt
-    wt_ref[...] = wt
-    sel = mt.T[:rows]
-    slot_gate = jnp.sum(wt.T[:rows], axis=1, keepdims=True)
-    sub_i = lax.broadcasted_iota(jnp.int32, (rows, 1), 0)
-    sub_exp = steps_of(sub_i, pack, n_sub)
-    sub_kind = steps_of(sub_i - sub_exp * pack, CAP, kinds + 1)
+    before = dot(picked.astype(BF16), as_mask(row_i < col_i))
+    placed = (before == sub_slot.astype(F32)) & (picked > 0.0) & (sub_kind < kinds)
+    sel = jnp.where(placed, 1.0, 0.0)
+    selw = jnp.where(placed, weight, 0.0)
+    sel_ref[...] = sel
+    selw_ref[...] = selw
+    slot_gate = jnp.sum(selw, axis=1, keepdims=True)
     is_cot = sub_kind == 1
     for h in range(1, halves):
         is_cot = is_cot | (sub_kind == 2 * h + 1)
-    row_scale = jnp.where(is_cot, slot_gate, 1.0)
+    row_scale = jnp.where(is_cot, jnp.broadcast_to(slot_gate, is_cot.shape), 1.0)[:, :1]
     takes = [jnp.where(sub_kind == x, sel, 0.0).astype(BF16) for x in range(kinds)]
 
     def columns(blk, h):
@@ -277,6 +277,8 @@
             part_send[db, :, m * ff : (m + 1) * ff] = value.astype(BF16)
         rs_copy(db).start()
 
+    for fetch in fetches:
+        fetch.wait()
     forward(1)
     for m, value in enumerate(partial(0)):
         part_own[:, m * ff : (m + 1) * ff] = value
@@ -385,52 +387,7 @@
     each(1, n_sub, lambda ds: bk_copy(ds).start())
     back[b, s] = fin[0, s]
 
-    x_all = xs[...].reshape(n_blk * chunk, d_blk)
-    do_all = dos[...].reshape(n_blk * chunk, d_blk)
-    gd_ref[0] = dot_tn(hid[:, :, :ff].reshape(n_blk * chunk, ff), do_all) * scale
-    gg_ref[0] = dot_tn(hid[:, :, ff : 2 * ff].reshape(n_blk * chunk, ff), x_all) * scale
-    gu_ref[0] = dot_tn(hid[:, :, 2 * ff :].reshape(n_blk * chunk, ff), x_all) * scale
-
-    wt_all = wt_ref[:, :rows]
-    wt_high = wt_all.astype(BF16)
-    wt_low = (wt_all - wt_high.astype(F32)).astype(BF16)
-    mt_low = mt_ref[:, :rows].astype(BF16)
-    kind_row = lane_kind[:, :rows]
-    none = jnp.zeros((tok_count, rows), BF16)
-
-    def collect(db, dots):
-        blk = wrap(b + db, n_blk)
-        got = back[blk].reshape(rows, width)
-        for h in range(halves):
-            cols = columns(blk, h)
-            high = jnp.where(kind_row == 2 * h, wt_high, none)
-            low = jnp.where(kind_row == 2 * h, wt_low, none)
-            ones = jnp.where(kind_row == 2 * h + 1, mt_low, none)
-            mixed_ref[:, cols] = (dot(high, got) + dot(low, got)).astype(BF16)
-            tgrad_ref[:, cols] = dot(ones, got).astype(BF16)
-        return dots + jnp.sum(cots[blk].astype(F32) * got.astype(F32), axis=1, keepdims=True)
-
-    each(1, n_sub, lambda ds: bk_copy(ds).wait_recv())
-    dots = collect(0, jnp.zeros((rows, 1), F32))
-
-    def step(db, dots):
-        each(0, n_sub, lambda ds: bk_copy(db * n_sub + ds).wait_recv())
-        return collect(db, dots)
-
-    if n_blk <= 8:
-        for db in range(1, n_blk):
-            dots = step(db, dots)
-    else:
-        dots = lax.fori_loop(1, n_blk, step, dots)
-    wide = jnp.broadcast_to(dots, (rows, tok_count))
-    if lanes > rows:
-        wide = jnp.concatenate([wide, jnp.zeros((lanes - rows, tok_count), F32)], axis=0)
-    token_dots = mt_ref[...] * wide.T
-    picks = []
-    for k in range(ids_ref.shape[1]):
-        hit = ids_ref[:, k : k + 1] == lane_exp
-        picks.append(jnp.sum(jnp.where(hit, token_dots, 0.0), axis=1, keepdims=True))
-    ggrad_ref[...] = jnp.concatenate(picks, axis=1)
+    each(1, n_blk * n_sub, lambda k: bk_copy(k).wait_recv())
 
     each(1, n_blk * n_sub, lambda k: disp_copy(k).wait_send())
     each(0, n_blk * n_sub, lambda k: fwd_copy(k).wait_send())
@@ -438,6 +395,92 @@
     each(1, n_blk, lambda db: ag_copy(db).wait_send())
     each(0, n_blk, lambda db: px_copy(db).wait_send())
     each(1, n_blk * n_sub, lambda k: bk_copy(k).wait_send())
+
+
+def finish_kernel(
+    dims,
+    ids_ref,
+    sel_ref,
+    selw_ref,
+    cots,
+    xs,
+    dos,
+    hid,
+    back,
+    mixed_hbm,
+    tgrad_hbm,
+    ggrad_hbm,
+    gg_hbm,
+    gu_hbm,
+    gd_hbm,
+    mixed_ref,
+    tgrad_ref,
+    ggrad_ref,
+    gg_ref,
+    gu_ref,
+    gd_ref,
+    sems,
+):
+    n_blk, n_sub, halves, pack, scale = dims
+    d_blk = xs.shape[2]
+    all_rows = n_blk * xs.shape[1]
+    ff = hid.shape[2] // 3
+    width = d_blk // halves
+    rows = n_sub * pack
+    kinds = 2 * halves
+    pairs = (
+        (mixed_ref, mixed_hbm),
+        (tgrad_ref, tgrad_hbm),
+        (ggrad_ref, ggrad_hbm),
+        (gg_ref, gg_hbm),
+        (gu_ref, gu_hbm),
+        (gd_ref, gd_hbm),
+    )
+    outs = [pltpu.make_async_copy(src, dst, sems.at[i]) for i, (src, dst) in enumerate(pairs)]
+    x_all = xs[...].reshape(all_rows, d_blk)
+    gg_ref[0] = dot_tn(hid[:, :, ff : 2 * ff].reshape(all_rows, ff), x_all) * scale
+    outs[3].start()
+    gu_ref[0] = dot_tn(hid[:, :, 2 * ff :].reshape(all_rows, ff), x_all) * scale
+    outs[4].start()
+    do_all = dos[...].reshape(all_rows, d_blk)
+    gd_ref[0] = dot_tn(hid[:, :, :ff].reshape(all_rows, ff), do_all) * scale
+    outs[5].start()
+
+    tok_count = sel_ref.shape[1]
+    sub_i = lax.broadcasted_iota(jnp.int32, (rows, tok_count), 0)
+    sub_exp = steps_of(sub_i, pack, n_sub)
+    sub_kind = steps_of(sub_i - sub_exp * pack, CAP, kinds + 1)
+    selw = selw_ref[...]
+    high = selw.astype(BF16).astype(F32)
+    low = selw - high
+    takes = []
+    for h in range(halves):
+        mine = sub_kind == 2 * h
+        takes.append(
+            [
+                jnp.where(mine, high, 0.0).T.astype(BF16),
+                jnp.where(mine, low, 0.0).T.astype(BF16),
+                jnp.where(sub_kind == 2 * h + 1, sel_ref[...], 0.0).T.astype(BF16),
+            ]
+        )
+    dots = jnp.zeros((rows, 1), F32)
+    for blk in range(n_blk):
+        got = back[blk].reshape(rows, width)
+        for h in range(halves):
+            cols = slice(blk * d_blk + h * width, blk * d_blk + (h + 1) * width)
+            high_t, low_t, ones_t = takes[h]
+            mixed_ref[:, cols] = (dot(high_t, got) + dot(low_t, got)).astype(BF16)
+            tgrad_ref[:, cols] = dot(ones_t, got).astype(BF16)
+        dots = dots + jnp.sum(cots[blk].astype(F32) * got.astype(F32), axis=1, keepdims=True)
+    outs[0].start()
+    outs[1].start()
+    token_dots = sel_ref[...] * dots
+    for k in range(ids_ref.shape[0]):
+        hit = ids_ref[k : k + 1, :] == sub_exp
+        ggrad_ref[k : k + 1, :] = jnp.sum(jnp.where(hit, token_dots, 0.0), axis=0, keepdims=True)
+    outs[2].start()
+    for out in outs:
+        out.wait()
 
 
 def on_device(tokens, expert_ids, gate_weights, w_gate, w_up, w_down, cotangent):
@@ -449,60 +492,76 @@
     width = d_blk // halves
     pack = -(-2 * halves * CAP // 16) * 16
     rows = n_sub * pack
-    lanes = -(-rows // 128) * 128
     chunk = n_sub * n_rep * CAP
     pairs = n_blk * n_sub
     dma = pltpu.SemaphoreType.DMA
     vmem = pl.BlockSpec(memory_space=pltpu.VMEM)
-    dims = (n_blk, n_sub, n_rep, halves, pack, scale)
-    grad = jax.ShapeDtypeStruct((1, ff, d_blk), F32)
-    return pl.pallas_call(
-        functools.partial(kernel, dims),
-        out_shape=(
-            jax.ShapeDtypeStruct((tok_count, d_model), BF16),
-            jax.ShapeDtypeStruct((tok_count, d_model), BF16),
-            jax.ShapeDtypeStruct(gate_weights.shape, F32),
-            grad,
-            grad,
-            grad,
-        ),
-        in_specs=[vmem] * 7,
-        out_specs=(vmem,) * 6,
-        scratch_shapes=[
-            pltpu.VMEM((tok_count, lanes), F32),
-            pltpu.VMEM((tok_count, lanes), F32),
-            pltpu.VMEM((n_blk, n_sub, pack, width), BF16),
-            pltpu.VMEM((pairs * n_rep, pack, width), BF16),
-            pltpu.VMEM((n_blk, rows, width), BF16),
-            pltpu.VMEM((n_blk, chunk, d_blk), BF16),
-            pltpu.VMEM((n_blk, chunk, d_blk), BF16),
-            pltpu.VMEM((chunk, 3 * ff), F32),
-            pltpu.VMEM((n_blk, chunk, 3 * ff), BF16),
-            pltpu.VMEM((n_blk, chunk, 3 * ff), BF16),
-            pltpu.VMEM((n_blk, chunk, 3 * ff), BF16),
-            pltpu.VMEM((n_blk, n_sub, pack, width), BF16),
-            pltpu.VMEM((n_blk, n_sub, pack, width), BF16),
-            pltpu.VMEM((n_blk, n_sub, pack, width), BF16),
-            pltpu.VMEM((n_blk, n_sub, pack, width), BF16),
-            pltpu.VMEM((n_blk, n_sub, pack, width), BF16),
-            dma((pairs,)),
-            dma((pairs,)),
-            dma((pairs,)),
-            dma((pairs,)),
-            dma((n_blk,)),
-            dma((n_blk,)),
-            dma((n_blk,)),
-            dma((n_blk,)),
-            dma((n_blk,)),
-            dma((n_blk,)),
-            dma((pairs,)),
-            dma((pairs,)),
-        ],
+    anywhere = pl.BlockSpec(memory_space=pl.ANY)
+    packed = (n_blk, n_sub, pack, width)
+    shaped = jax.ShapeDtypeStruct
+    handed = (
+        shaped((rows, tok_count), F32),
+        shaped((rows, tok_count), F32),
+        shaped((n_blk, rows, width), BF16),
+        shaped((n_blk, chunk, d_blk), BF16),
+        shaped((n_blk, chunk, d_blk), BF16),
+        shaped((n_blk, chunk, 3 * ff), BF16),
+        shaped(packed, BF16),
+    )
+    held = [
+        ((1, ff, d_blk), BF16),
+        ((1, ff, d_blk), BF16),
+        ((1, ff, d_blk), BF16),
+        (packed, BF16),
+        ((pairs * n_rep, pack, width), BF16),
+        ((chunk, 3 * ff), F32),
+        ((n_blk, chunk, 3 * ff), BF16),
+        ((n_blk, chunk, 3 * ff), BF16),
+        (packed, BF16),
+        (packed, BF16),
+        (packed, BF16),
+        (packed, BF16),
+    ]
+    inside = sum(math.prod(shape) * jnp.dtype(kind).itemsize for shape, kind in held)
+    inside += sum(math.prod(one.shape) * one.dtype.itemsize for one in handed)
+    ids, gates = expert_ids.T, gate_weights.T
+    between = pl.pallas_call(
+        functools.partial(kernel, (n_blk, n_sub, n_rep, halves, pack)),
+        out_shape=handed,
+        in_specs=[vmem] * 4 + [anywhere] * 3,
+        out_specs=(vmem,) * len(handed),
+        scratch_shapes=[pltpu.VMEM(shape, kind) for shape, kind in held]
+        + [dma((3,))]
+        + [dma((pairs,))] * 4
+        + [dma((n_blk,))] * 6
+        + [dma((pairs,))] * 2,
         compiler_params=pltpu.CompilerParams(
-            collective_id=0, has_side_effects=True, vmem_limit_bytes=56 * 1024 * 1024
+            collective_id=0,
+            has_side_effects=True,
+            vmem_limit_bytes=(12 << 20) + inside + inside // 4,
         ),
         cost_estimate=pl.CostEstimate(flops=1 << 30, bytes_accessed=8 << 20, transcendentals=chunk * ff),
-    )(expert_ids, gate_weights, tokens, cotangent, w_gate, w_up, w_down)
+    )(ids, gates, tokens, cotangent, w_gate, w_up, w_down)
+    grad = shaped((1, ff, d_blk), F32)
+    results = (
+        shaped((tok_count, d_model), BF16),
+        shaped((tok_count, d_model), BF16),
+        shaped(gates.shape, F32),
+        grad,
+        grad,
+        grad,
+    )
+    room = sum(math.prod(one.shape) * one.dtype.itemsize for one in handed + results)
+    mixed, token_grad, gate_grad, grad_gate, grad_up, grad_down = pl.pallas_call(
+        functools.partial(finish_kernel, (n_blk, n_sub, halves, pack, scale)),
+        out_shape=results,
+        in_specs=[vmem] * (1 + len(handed)),
+        out_specs=(anywhere,) * len(results),
+        scratch_shapes=[pltpu.VMEM(one.shape, one.dtype) for one in results] + [dma((len(results),))],
+        compiler_params=pltpu.CompilerParams(vmem_limit_bytes=(12 << 20) + room + room // 4),
+        cost_estimate=pl.CostEstimate(flops=1 << 28, bytes_accessed=5 << 20, transcendentals=0),
+    )(ids, *between)
+    return mixed, token_grad, gate_grad.T, grad_gate, grad_up, grad_down
 
 
 def solution(mesh):

time: 58.7 us -> 54.1 us (0.922)
  local copies, waits for them, and re-layouts: 10.2 us -> 6.43 us
  Pallas kernels: 47.5 us -> 46.6 us
    unnamed x17 -> x14, local copies, waits for them, and re-layouts: 8.62 us -> 6.43 us
    pallas_call x1 -> x0, local copies, waits for them, and re-layouts: 1.56 us -> none  [on_device(): pl.pallas_call(functools.partial(kernel, dims), out_shape=(jax.ShapeDtype...]
    pallas_call x1 -> x2, Pallas kernels: 47.5 us -> 46.6 us  [the longest x1 44 us: on_device(): pl.pallas_call(functools.partial(kernel, (n_blk, n_sub, n_rep, halves, pa...]
where the time goes in v2:
time: 54.1 us; the launch traced here: 53.7 us
  Pallas kernels  46.6 us (86%)
  local copies, waits for them, and re-layouts  6.43 us (12%)
  between operations  0.66 us (1%)
    pallas_call x1, Pallas kernels, on_device(): pl.pallas_call(functools.partial(kernel, (n_blk, n_sub, n_rep, halves, pa...  44 us
    unnamed x14, local copies, waits for them, and re-layouts  6.43 us
    pallas_call x1, Pallas kernels, on_device(): pl.pallas_call(functools.partial(finish_kernel, (n_blk, n_sub, halves, pa...  2.62 us

profile of v2, /device:TPU:0, one launch (start us, length us, event | category | flops | bytes accessed | tf_op | source)
XLA Modules:
  0.0 53.7 jit_solution(1692073569061951631)
XLA Ops:
  0.6 0.0 copy-start
  0.6 0.7 %copy-done = s32[128,8]{0,1:T(8,128)S(1)} copy-done((s32[128,8]{0,1:T(8,128)S(1)}, s32[128,8]{0,1:T(8,128)}, u32[]{:S(2)}) %copy-start) | copy-done | bytes 4120
  1.3 0.0 copy-start.1
  1.3 1.0 %copy-done.1 = bf16[128,2048]{1,0:T(8,128)(2,1)S(1)} copy-done((bf16[128,2048]{1,0:T(8,128)(2,1)S(1)}, bf16[128,2048]{1,0:T(8,128)(2,1)}, u32[]{:S(2)}) %copy-start.1) | copy-done | bytes 524312
  2.4 0.0 copy-start.2
  2.4 1.0 %copy-done.2 = bf16[128,2048]{1,0:T(8,128)(2,1)S(1)} copy-done((bf16[128,2048]{1,0:T(8,128)(2,1)S(1)}, bf16[128,2048]{1,0:T(8,128)(2,1)}, u32[]{:S(2)}) %copy-start.2) | copy-done | bytes 524312
  3.4 0.0 copy-start.3
  3.4 1.0 %copy-done.3 = bf16[1,384,512]{2,1,0:T(8,128)(2,1)S(1)} copy-done((bf16[1,384,512]{2,1,0:T(8,128)(2,1)S(1)}, bf16[1,384,512]{2,1,0:T(8,128)(2,1)}, u32[]{:S(2)}) %copy-start.3) | copy-done | bytes 393240
  4.4 0.0 copy-start.4
  4.4 1.0 %copy-done.4 = bf16[1,384,512]{2,1,0:T(8,128)(2,1)S(1)} copy-done((bf16[1,384,512]{2,1,0:T(8,128)(2,1)S(1)}, bf16[1,384,512]{2,1,0:T(8,128)(2,1)}, u32[]{:S(2)}) %copy-start.4) | copy-done | bytes 393240
  5.4 0.0 copy-start.5
  5.4 1.0 %copy-done.5 = bf16[1,384,512]{2,1,0:T(8,128)(2,1)S(1)} copy-done((bf16[1,384,512]{2,1,0:T(8,128)(2,1)S(1)}, bf16[1,384,512]{2,1,0:T(8,128)(2,1)}, u32[]{:S(2)}) %copy-start.5) | copy-done | bytes 393240
  6.4 0.0 copy-start.6
  6.4 0.7 %copy-done.6 = f32[128,8]{0,1:T(8,128)S(1)} copy-done((f32[128,8]{0,1:T(8,128)S(1)}, f32[128,8]{0,1:T(8,128)}, u32[]{:S(2)}) %copy-start.6) | copy-done | bytes 4120
  7.1 44.0 %shard_map.118 = (f32[96,128]{1,0:T(8,128)S(1)}, f32[96,128]{1,0:T(8,128)S(1)}, bf16[4,96,256]{2,1,0:T(8,128)(2,1)S(1)}, bf16[4,48,512]{2,1,0:T(8,128)(2,1)S(1)}...) custom-call(s32[8,128]{1,0:T(8,128)S(1)} %bitcast.3, ...), custom_call_target="tpu_custom_call" | custom-call | flops 1073741824 | bytes 8388608 | tf_op jit(solution)/shard_map/pallas_call | solution.py:528
  51.1 2.6 %shard_map.119 = (bf16[128,2048]{1,0:T(8,128)(2,1)}, bf16[128,2048]{1,0:T(8,128)(2,1)}, f32[8,128]{1,0:T(8,128)}, f32[1,384,512]{2,1,0:T(8,128)}, f32[1,384,512]{2,1,0:T(8,128)}, /*index=5*/f32[1,384,512]{2,1,0:T(8,128)}) custom-call(s32[8,128]{1,0:T(8,128)S(1)} %bitcast.4, f32[96,128]{1,0:T(8,128)S(1)} %get-tuple-element.19.sel_ref, ...), custom_call_target="tpu_custom_call" | custom-call | flops 268435456 | bytes 5242880 | tf_op jit(solution)/shard_map/pallas_call | solution.py:555
Async XLA Ops:
  0.6 0.7 %copy-start = (s32[128,8]{0,1:T(8,128)S(1)}, s32[128,8]{0,1:T(8,128)}, u32[]{:S(2)}) copy-start(s32[128,8]{0,1:T(8,128)} %param.8) | copy-start | bytes 12292
  1.3 1.0 %copy-start.1 = (bf16[128,2048]{1,0:T(8,128)(2,1)S(1)}, bf16[128,2048]{1,0:T(8,128)(2,1)}, u32[]{:S(2)}) copy-start(bf16[128,2048]{1,0:T(8,128)(2,1)} %tok_ref.1) | copy-start | bytes 1572868
  2.4 1.0 %copy-start.2 = (bf16[128,2048]{1,0:T(8,128)(2,1)S(1)}, bf16[128,2048]{1,0:T(8,128)(2,1)}, u32[]{:S(2)}) copy-start(bf16[128,2048]{1,0:T(8,128)(2,1)} %cot_ref.1) | copy-start | bytes 1572868
  3.4 1.0 %copy-start.3 = (bf16[1,384,512]{2,1,0:T(8,128)(2,1)S(1)}, bf16[1,384,512]{2,1,0:T(8,128)(2,1)}, u32[]{:S(2)}) copy-start(bf16[1,384,512]{2,1,0:T(8,128)(2,1)} %wg_hbm.1) | copy-start | bytes 1179652
  4.4 1.0 %copy-start.4 = (bf16[1,384,512]{2,1,0:T(8,128)(2,1)S(1)}, bf16[1,384,512]{2,1,0:T(8,128)(2,1)}, u32[]{:S(2)}) copy-start(bf16[1,384,512]{2,1,0:T(8,128)(2,1)} %wu_hbm.1) | copy-start | bytes 1179652
  5.4 1.0 %copy-start.5 = (bf16[1,384,512]{2,1,0:T(8,128)(2,1)S(1)}, bf16[1,384,512]{2,1,0:T(8,128)(2,1)}, u32[]{:S(2)}) copy-start(bf16[1,384,512]{2,1,0:T(8,128)(2,1)} %wd_hbm.1) | copy-start | bytes 1179652
  6.4 0.7 %copy-start.6 = (f32[128,8]{0,1:T(8,128)S(1)}, f32[128,8]{0,1:T(8,128)}, u32[]{:S(2)}) copy-start(f32[128,8]{0,1:T(8,128)} %param.9) | copy-start | bytes 12292

commit v3 on v2

--- a/solution.py
+++ b/solution.py
@@ -1,5 +1,4 @@
 import functools
-import math
 
 import jax
 import jax.numpy as jnp
@@ -11,6 +10,7 @@
 NUM_EXPERTS = 128
 TOPK = 8
 CAP = 12
+VMEM_LIMIT = 60 << 20
 MESH = pl.DeviceIdType.MESH
 BF16 = jnp.bfloat16
 F32 = jnp.float32
@@ -60,13 +60,14 @@
 
 def kernel(
     dims,
-    ids_ref,
-    gw_ref,
-    tok_ref,
-    cot_ref,
+    ids_hbm,
+    gw_hbm,
+    tok_hbm,
+    cot_hbm,
     wg_hbm,
     wu_hbm,
     wd_hbm,
+    ids_ref,
     sel_ref,
     selw_ref,
     cots,
@@ -74,6 +75,9 @@
     dos,
     hid,
     back,
+    gw_ref,
+    tok_ref,
+    cot_ref,
     wg_ref,
     wu_ref,
     wd_ref,
@@ -86,7 +90,7 @@
     px_send,
     px_recv,
     fin,
-    w_s,
+    in_s,
     disp_s,
     disp_r,
     fwd_s,
@@ -95,6 +99,7 @@
     rs_r,
     ag_s,
     ag_r,
+    ag_l,
     px_s,
     px_r,
     bk_s,
@@ -109,6 +114,8 @@
     chunk = per_blk * CAP
     rows = n_sub * pack
     kinds = 2 * halves
+    pieces = hid.shape[1]
+    unit = ff // pieces
     b = lax.axis_index("blk")
     s = lax.axis_index("sub")
     r = lax.axis_index("rep")
@@ -117,10 +124,16 @@
     def wrap(v, n):
         return lax.rem(v + n, n)
 
-    fetches = [
-        pltpu.make_async_copy(src, dst, w_s.at[i])
-        for i, (src, dst) in enumerate(((wg_hbm, wg_ref), (wu_hbm, wu_ref), (wd_hbm, wd_ref)))
-    ]
+    operands = (
+        (ids_hbm, ids_ref),
+        (gw_hbm, gw_ref),
+        (tok_hbm, tok_ref),
+        (cot_hbm, cot_ref),
+        (wg_hbm, wg_ref),
+        (wu_hbm, wu_ref),
+        (wd_hbm, wd_ref),
+    )
+    fetches = [pltpu.make_async_copy(src, dst, in_s.at[i]) for i, (src, dst) in enumerate(operands)]
     for fetch in fetches:
         fetch.start()
 
@@ -138,6 +151,9 @@
         )
 
     each(1, group, greet)
+
+    for fetch in fetches[:2]:
+        fetch.wait()
 
     sub_i = lax.broadcasted_iota(jnp.int32, (rows, tok_count), 0)
     sub_exp = steps_of(sub_i, pack, n_sub)
@@ -206,6 +222,8 @@
     def send_rows(db):
         each(0, n_sub, lambda ds: disp_copy(db * n_sub + ds).start())
 
+    for fetch in fetches[2:4]:
+        fetch.wait()
     gather(1)
     pl.semaphore_wait(barrier, group - 1)
     send_rows(1)
@@ -252,12 +270,12 @@
 
     each(0, n_blk, cot_rows)
 
-    def rs_copy(db):
+    def rs_copy(db, p):
         return pltpu.make_async_remote_copy(
-            src_ref=part_send.at[db],
-            dst_ref=part_recv.at[db],
-            send_sem=rs_s.at[db],
-            recv_sem=rs_r.at[db],
+            src_ref=part_send.at[db, p],
+            dst_ref=part_recv.at[db, p],
+            send_sem=rs_s.at[db * pieces + p],
+            recv_sem=rs_r.at[db * pieces + p],
             device_id={"blk": wrap(b - db, n_blk)},
             device_id_type=MESH,
         )
@@ -273,15 +291,18 @@
         return dot_nt(x, wg_ref[0]), dot_nt(x, wu_ref[0]), dot_nt(do, wd_ref[0])
 
     def partial_send(db):
-        for m, value in enumerate(partial(db)):
-            part_send[db, :, m * ff : (m + 1) * ff] = value.astype(BF16)
-        rs_copy(db).start()
-
-    for fetch in fetches:
+        values = partial(db)
+        for p in range(pieces):
+            for m, value in enumerate(values):
+                part_send[db, p, :, m * unit : (m + 1) * unit] = value[:, p * unit : (p + 1) * unit].astype(BF16)
+            rs_copy(db, p).start()
+
+    for fetch in fetches[4:]:
         fetch.wait()
     forward(1)
     for m, value in enumerate(partial(0)):
-        part_own[:, m * ff : (m + 1) * ff] = value
+        for p in range(pieces):
+            part_own[p, :, m * unit : (m + 1) * unit] = value[:, p * unit : (p + 1) * unit]
 
     def middle(db):
         forward(db + 1)
@@ -290,32 +311,75 @@
     each(1, n_blk - 1, middle)
     partial_send(n_blk - 1)
 
-    def add_part(db):
-        rs_copy(db).wait_recv()
-        part_own[...] += part_recv[db].astype(F32)
-
-    each(1, n_blk, add_part)
-    pre_gate = part_own[:, :ff]
-    pre_up = part_own[:, ff : 2 * ff]
-    dhid = part_own[:, 2 * ff :]
-    sig = jax.nn.sigmoid(pre_gate)
-    act = pre_gate * sig
-    slope = sig * (1.0 + pre_gate * (1.0 - sig))
-    hid[b, :, :ff] = (act * pre_up).astype(BF16)
-    hid[b, :, ff : 2 * ff] = (dhid * pre_up * slope).astype(BF16)
-    hid[b, :, 2 * ff :] = (dhid * act).astype(BF16)
-
-    def ag_copy(db):
+    def ag_copy(c, p, to, sem):
         return pltpu.make_async_remote_copy(
-            src_ref=hid.at[b],
-            dst_ref=hid.at[b],
-            send_sem=ag_s.at[db],
-            recv_sem=ag_r.at[db],
-            device_id={"blk": wrap(b + db, n_blk)},
-            device_id_type=MESH,
-        )
-
-    each(1, n_blk, lambda db: ag_copy(db).start())
+            src_ref=hid.at[c, p],
+            dst_ref=hid.at[c, p],
+            send_sem=sem,
+            recv_sem=ag_r.at[c * pieces + p],
+            device_id={"blk": to},
+            device_id_type=MESH,
+        )
+
+    def to_right(p):
+        return ag_copy(b, p, wrap(b + 1, n_blk), ag_s.at[b * pieces + p])
+
+    def to_left(p):
+        return ag_copy(b, p, wrap(b - 1, n_blk), ag_l.at[p])
+
+    def both_ways(p, act):
+        @pl.when(b + 1 < n_blk)
+        def _():
+            act(to_right(p))
+
+        @pl.when(b >= 1)
+        def _():
+            act(to_left(p))
+
+    for p in range(pieces):
+
+        def add_part(db):
+            rs_copy(db, p).wait_recv()
+            part_own[p] += part_recv[db, p].astype(F32)
+
+        each(1, n_blk, add_part)
+        pre_gate = part_own[p, :, :unit]
+        pre_up = part_own[p, :, unit : 2 * unit]
+        dhid = part_own[p, :, 2 * unit :]
+        sig = jax.nn.sigmoid(pre_gate)
+        act = pre_gate * sig
+        slope = sig * (1.0 + pre_gate * (1.0 - sig))
+        hid[b, p, :, :unit] = (act * pre_up).astype(BF16)
+        hid[b, p, :, unit : 2 * unit] = (dhid * pre_up * slope).astype(BF16)
+        hid[b, p, :, 2 * unit :] = (dhid * act).astype(BF16)
+        both_ways(p, lambda copy: copy.start())
+
+    def pass_copy(c, p, step):
+        return ag_copy(c, p, wrap(b + step, n_blk), ag_s.at[c * pieces + p])
+
+    def take(c, step):
+        for p in range(pieces):
+            pass_copy(c, p, step).wait_recv()
+
+            @pl.when((b + step >= 0) & (b + step < n_blk))
+            def _():
+                pass_copy(c, p, step).start()
+
+    def passed(c, step):
+        for p in range(pieces):
+
+            @pl.when((b + step >= 0) & (b + step < n_blk))
+            def _():
+                pass_copy(c, p, step).wait_send()
+
+    def at_distance(d, fn):
+        @pl.when(b - d >= 0)
+        def _():
+            fn(b - d, 1)
+
+        @pl.when(b + d < n_blk)
+        def _():
+            fn(b + d, -1)
 
     srow = lax.broadcasted_iota(jnp.int32, (rows, chunk), 0)
     scol = lax.broadcasted_iota(jnp.int32, (rows, chunk), 1)
@@ -330,33 +394,44 @@
 
     to_mine, to_other = repack(r), repack(other)
 
-    def px_copy(db):
+    def px_copy(c):
         return pltpu.make_async_remote_copy(
-            src_ref=px_send.at[db],
-            dst_ref=px_recv.at[db],
-            send_sem=px_s.at[db],
-            recv_sem=px_r.at[db],
+            src_ref=px_send.at[c],
+            dst_ref=px_recv.at[c],
+            send_sem=px_s.at[c],
+            recv_sem=px_r.at[c],
             device_id={"rep": other},
             device_id_type=MESH,
         )
 
-    def bk_copy(k):
+    def bk_copy(c, dst_s):
+        return pltpu.make_async_remote_copy(
+            src_ref=fin.at[c, dst_s],
+            dst_ref=back.at[b, s],
+            send_sem=bk_s.at[c * n_sub + dst_s],
+            recv_sem=bk_r.at[b * n_sub + s],
+            device_id={"blk": c, "sub": dst_s},
+            device_id_type=MESH,
+        )
+
+    def bk_arrival(k):
         db, ds = div_mod(k, n_sub)
-        dst_s = wrap(s + ds, n_sub)
+        from_b, from_s = wrap(b + db, n_blk), wrap(s + ds, n_sub)
         return pltpu.make_async_remote_copy(
-            src_ref=fin.at[db, dst_s],
-            dst_ref=back.at[b, s],
-            send_sem=bk_s.at[k],
-            recv_sem=bk_r.at[k],
-            device_id={"blk": wrap(b - db, n_blk), "sub": dst_s},
-            device_id_type=MESH,
-        )
-
-    def outputs(db):
-        blk = wrap(b - db, n_blk)
-        out = dot(hid[blk, :, :ff], wd_ref[0]).astype(BF16)
-        into = dot(hid[blk, :, ff : 2 * ff], wg_ref[0]) + dot(hid[blk, :, 2 * ff :], wu_ref[0])
-        into = into.astype(BF16)
+            src_ref=fin.at[from_b, from_s],
+            dst_ref=back.at[from_b, from_s],
+            send_sem=bk_s.at[from_b * n_sub + from_s],
+            recv_sem=bk_r.at[from_b * n_sub + from_s],
+            device_id={"blk": from_b, "sub": from_s},
+            device_id_type=MESH,
+        )
+
+    def outputs(c, step):
+        def whole(m):
+            return jnp.concatenate([hid[c, p, :, m * unit : (m + 1) * unit] for p in range(pieces)], axis=1)
+
+        out = dot(whole(0), wd_ref[0]).astype(BF16)
+        into = (dot(whole(1), wg_ref[0]) + dot(whole(2), wu_ref[0])).astype(BF16)
 
         def packed(masks):
             acc = None
@@ -366,47 +441,49 @@
                 acc = term if acc is None else acc + term
             return acc.astype(BF16).reshape(n_sub, pack, width)
 
-        px_send[db] = packed(to_other)
-        px_copy(db).start()
-        px_own[db] = packed(to_mine)
-
-    def finish(db):
-        px_copy(db).wait_recv()
-        fin[db] = (px_own[db].astype(F32) + px_recv[db].astype(F32)).astype(BF16)
-
-    outputs(0)
-
-    def rest(db):
-        ag_copy(db).wait_recv()
-        outputs(db)
-        finish(db)
-        each(0, n_sub, lambda ds: bk_copy(db * n_sub + ds).start())
+        px_send[c] = packed(to_other)
+        px_copy(c).start()
+        px_own[c] = packed(to_mine)
+
+    def finish(c, step):
+        px_copy(c).wait_recv()
+        fin[c] = (px_own[c].astype(F32) + px_recv[c].astype(F32)).astype(BF16)
+        each(0, n_sub, lambda dst_s: bk_copy(c, dst_s).start())
+
+    outputs(b, 0)
+
+    def rest(d):
+        at_distance(d, take)
+        at_distance(d, outputs)
+        at_distance(d, finish)
 
     each(1, n_blk, rest)
-    finish(0)
-    each(1, n_sub, lambda ds: bk_copy(ds).start())
-    back[b, s] = fin[0, s]
-
-    each(1, n_blk * n_sub, lambda k: bk_copy(k).wait_recv())
+    px_copy(b).wait_recv()
+    fin[b] = (px_own[b].astype(F32) + px_recv[b].astype(F32)).astype(BF16)
+    each(1, n_sub, lambda ds: bk_copy(b, wrap(s + ds, n_sub)).start())
+    back[b, s] = fin[b, s]
+    each(1, n_blk * n_sub, lambda k: bk_arrival(k).wait_recv())
 
     each(1, n_blk * n_sub, lambda k: disp_copy(k).wait_send())
     each(0, n_blk * n_sub, lambda k: fwd_copy(k).wait_send())
-    each(1, n_blk, lambda db: rs_copy(db).wait_send())
-    each(1, n_blk, lambda db: ag_copy(db).wait_send())
-    each(0, n_blk, lambda db: px_copy(db).wait_send())
-    each(1, n_blk * n_sub, lambda k: bk_copy(k).wait_send())
+    for p in range(pieces):
+        each(1, n_blk, lambda db: rs_copy(db, p).wait_send())
+        both_ways(p, lambda copy: copy.wait_send())
+    each(1, n_blk, lambda d: at_distance(d, passed))
+    each(0, n_blk, lambda c: px_copy(c).wait_send())
+    each(1, n_blk * n_sub, lambda k: bk_arrival(k).wait_send())
 
 
 def finish_kernel(
     dims,
-    ids_ref,
-    sel_ref,
-    selw_ref,
-    cots,
-    xs,
-    dos,
-    hid,
-    back,
+    ids_hbm,
+    sel_hbm,
+    selw_hbm,
+    cots_hbm,
+    xs_hbm,
+    dos_hbm,
+    hid_hbm,
+    back_hbm,
     mixed_hbm,
     tgrad_hbm,
     ggrad_hbm,
@@ -419,12 +496,21 @@
     gg_ref,
     gu_ref,
     gd_ref,
+    ids_ref,
+    sel_ref,
+    selw_ref,
+    cots,
+    xs,
+    dos,
+    hid,
+    back,
     sems,
+    in_sems,
 ):
     n_blk, n_sub, halves, pack, scale = dims
     d_blk = xs.shape[2]
     all_rows = n_blk * xs.shape[1]
-    ff = hid.shape[2] // 3
+    pieces, unit = hid.shape[1], hid.shape[3] // 3
     width = d_blk // halves
     rows = n_sub * pack
     kinds = 2 * halves
@@ -437,15 +523,38 @@
         (gd_ref, gd_hbm),
     )
     outs = [pltpu.make_async_copy(src, dst, sems.at[i]) for i, (src, dst) in enumerate(pairs)]
+    operands = (
+        (xs_hbm, xs),
+        (hid_hbm, hid),
+        (dos_hbm, dos),
+        (ids_hbm, ids_ref),
+        (sel_hbm, sel_ref),
+        (selw_hbm, selw_ref),
+        (cots_hbm, cots),
+        (back_hbm, back),
+    )
+    fetches = [pltpu.make_async_copy(src, dst, in_sems.at[i]) for i, (src, dst) in enumerate(operands)]
+    for fetch in fetches:
+        fetch.start()
+    for fetch in fetches[:3]:
+        fetch.wait()
     x_all = xs[...].reshape(all_rows, d_blk)
-    gg_ref[0] = dot_tn(hid[:, :, ff : 2 * ff].reshape(all_rows, ff), x_all) * scale
+    do_all = dos[...].reshape(all_rows, d_blk)
+
+    def weight_grad(m, right, out_ref):
+        for p in range(pieces):
+            left = hid[:, p, :, m * unit : (m + 1) * unit].reshape(all_rows, unit)
+            out_ref[0, p * unit : (p + 1) * unit, :] = dot_tn(left, right) * scale
+
+    weight_grad(1, x_all, gg_ref)
     outs[3].start()
-    gu_ref[0] = dot_tn(hid[:, :, 2 * ff :].reshape(all_rows, ff), x_all) * scale
+    weight_grad(2, x_all, gu_ref)
     outs[4].start()
-    do_all = dos[...].reshape(all_rows, d_blk)
-    gd_ref[0] = dot_tn(hid[:, :, :ff].reshape(all_rows, ff), do_all) * scale
+    weight_grad(0, do_all, gd_ref)
     outs[5].start()
 
+    for fetch in fetches[3:]:
+        fetch.wait()
     tok_count = sel_ref.shape[1]
     sub_i = lax.broadcasted_iota(jnp.int32, (rows, tok_count), 0)
     sub_exp = steps_of(sub_i, pack, n_sub)
@@ -499,46 +608,52 @@
     anywhere = pl.BlockSpec(memory_space=pl.ANY)
     packed = (n_blk, n_sub, pack, width)
     shaped = jax.ShapeDtypeStruct
+    pieces = ff // 128 if ff % 128 == 0 else 1
+    spread = (n_blk, pieces, chunk, 3 * ff // pieces)
+    ids, gates = expert_ids.T, gate_weights.T
     handed = (
+        shaped(ids.shape, ids.dtype),
         shaped((rows, tok_count), F32),
         shaped((rows, tok_count), F32),
         shaped((n_blk, rows, width), BF16),
         shaped((n_blk, chunk, d_blk), BF16),
         shaped((n_blk, chunk, d_blk), BF16),
-        shaped((n_blk, chunk, 3 * ff), BF16),
+        shaped(spread, BF16),
         shaped(packed, BF16),
     )
     held = [
+        (gates.shape, F32),
+        (tokens.shape, BF16),
+        (tokens.shape, BF16),
         ((1, ff, d_blk), BF16),
         ((1, ff, d_blk), BF16),
         ((1, ff, d_blk), BF16),
         (packed, BF16),
         ((pairs * n_rep, pack, width), BF16),
-        ((chunk, 3 * ff), F32),
-        ((n_blk, chunk, 3 * ff), BF16),
-        ((n_blk, chunk, 3 * ff), BF16),
+        (spread[1:], F32),
+        (spread, BF16),
+        (spread, BF16),
         (packed, BF16),
         (packed, BF16),
         (packed, BF16),
         (packed, BF16),
     ]
-    inside = sum(math.prod(shape) * jnp.dtype(kind).itemsize for shape, kind in held)
-    inside += sum(math.prod(one.shape) * one.dtype.itemsize for one in handed)
-    ids, gates = expert_ids.T, gate_weights.T
     between = pl.pallas_call(
         functools.partial(kernel, (n_blk, n_sub, n_rep, halves, pack)),
         out_shape=handed,
-        in_specs=[vmem] * 4 + [anywhere] * 3,
+        in_specs=[pl.BlockSpec(memory_space=pltpu.HBM)] * 7,
         out_specs=(vmem,) * len(handed),
         scratch_shapes=[pltpu.VMEM(shape, kind) for shape, kind in held]
-        + [dma((3,))]
+        + [dma((7,))]
         + [dma((pairs,))] * 4
-        + [dma((n_blk,))] * 6
+        + [dma((n_blk * pieces,))] * 4
+        + [dma((pieces,))]
+        + [dma((n_blk,))] * 2
         + [dma((pairs,))] * 2,
         compiler_params=pltpu.CompilerParams(
             collective_id=0,
             has_side_effects=True,
-            vmem_limit_bytes=(12 << 20) + inside + inside // 4,
+            vmem_limit_bytes=VMEM_LIMIT,
         ),
         cost_estimate=pl.CostEstimate(flops=1 << 30, bytes_accessed=8 << 20, transcendentals=chunk * ff),
     )(ids, gates, tokens, cotangent, w_gate, w_up, w_down)
@@ -551,16 +666,16 @@
         grad,
         grad,
     )
-    room = sum(math.prod(one.shape) * one.dtype.itemsize for one in handed + results)
     mixed, token_grad, gate_grad, grad_gate, grad_up, grad_down = pl.pallas_call(
         functools.partial(finish_kernel, (n_blk, n_sub, halves, pack, scale)),
         out_shape=results,
-        in_specs=[vmem] * (1 + len(handed)),
+        in_specs=[anywhere] * len(handed),
         out_specs=(anywhere,) * len(results),
-        scratch_shapes=[pltpu.VMEM(one.shape, one.dtype) for one in results] + [dma((len(results),))],
-        compiler_params=pltpu.CompilerParams(vmem_limit_bytes=(12 << 20) + room + room // 4),
+        scratch_shapes=[pltpu.VMEM(one.shape, one.dtype) for one in results + handed]
+        + [dma((len(results),)), dma((len(handed),))],
+        compiler_params=pltpu.CompilerParams(vmem_limit_bytes=VMEM_LIMIT),
         cost_estimate=pl.CostEstimate(flops=1 << 28, bytes_accessed=5 << 20, transcendentals=0),
-    )(ids, *between)
+    )(*between)
     return mixed, token_grad, gate_grad.T, grad_gate, grad_up, grad_down
 
 

time: 54.1 us -> 46 us (0.85)
  local copies, waits for them, and re-layouts: 6.43 us -> 0 us
  Pallas kernels: 46.6 us -> 45.2 us
    unnamed x14 -> x0, local copies, waits for them, and re-layouts: 6.43 us -> none
    pallas_call x1, Pallas kernels: 44 us -> 41.8 us  [on_device(): pl.pallas_call(functools.partial(kernel, (n_blk, n_sub, n_rep, halves, pa...]
    pallas_call x1, Pallas kernels: 2.62 us -> 3.4 us  [on_device(): pl.pallas_call(functools.partial(finish_kernel, (n_blk, n_sub, halves, pa...]
where the time goes in v3:
time: 46 us; the launch traced here: 45.9 us
  Pallas kernels  45.2 us (98%)
  between operations  0.64 us (1%)
    pallas_call x1, Pallas kernels, on_device(): pl.pallas_call(functools.partial(kernel, (n_blk, n_sub, n_rep, halves, pa...  41.8 us
    pallas_call x1, Pallas kernels, on_device(): pl.pallas_call(functools.partial(finish_kernel, (n_blk, n_sub, halves, pa...  3.4 us

profile of v3, /device:TPU:0, one launch (start us, length us, event | category | flops | bytes accessed | tf_op | source)
XLA Modules:
  0.0 45.9 jit_solution(16032529577219983077)
XLA Ops:
  0.6 41.8 %shard_map.118 = (s32[8,128]{1,0:T(8,128)}, f32[96,128]{1,0:T(8,128)}, f32[96,128]{1,0:T(8,128)}, bf16[4,96,256]{2,1,0:T(8,128)(2,1)}, bf16[4,48,512]{2,1,0:T(8,...) custom-call(s32[8,128]{1,0:T(8,128)} %bitcast.3, ...), custom_call_target="tpu_custom_call" | custom-call | flops 1073741824 | bytes 8388608 | tf_op jit(solution)/shard_map/pallas_call | solution.py:641
  42.4 3.4 %shard_map.119 = (bf16[128,2048]{1,0:T(8,128)(2,1)}, bf16[128,2048]{1,0:T(8,128)(2,1)}, f32[8,128]{1,0:T(8,128)}, f32[1,384,512]{2,1,0:T(8,128)}, f32[1,384,512]{2,1,0:T(8,128)}, /*index=5*/f32[1,384,512]{2,1,0:T(8,128)}) custom-call(s32[8,128]{1,0:T(8,128)} %get-tuple-element.20.ids_hbm, f32[96,128]{1,0:T(8,128)} %get-tuple-element.21.sel_hbm, ...), custom_call_target="tpu_custom_call" | custom-call | flops 268435456 | bytes 5242880 | tf_op jit(solution)/shard_map/pallas_call | solution.py:669

commit v4 on v3

--- a/solution.py
+++ b/solution.py
@@ -85,7 +85,8 @@
     recv1,
     part_own,
     part_send,
-    part_recv,
+    part_from_left,
+    part_from_right,
     px_own,
     px_send,
     px_recv,
@@ -96,7 +97,8 @@
     fwd_s,
     fwd_r,
     rs_s,
-    rs_r,
+    rs_left,
+    rs_right,
     ag_s,
     ag_r,
     ag_l,
@@ -270,13 +272,14 @@
 
     each(0, n_blk, cot_rows)
 
-    def rs_copy(db, p):
+    def rs_copy(c, p, step):
+        land, sems = (part_from_left, rs_left) if step == 1 else (part_from_right, rs_right)
         return pltpu.make_async_remote_copy(
-            src_ref=part_send.at[db, p],
-            dst_ref=part_recv.at[db, p],
-            send_sem=rs_s.at[db * pieces + p],
-            recv_sem=rs_r.at[db * pieces + p],
-            device_id={"blk": wrap(b - db, n_blk)},
+            src_ref=part_send.at[c, p],
+            dst_ref=land.at[c, p],
+            send_sem=rs_s.at[c * pieces + p],
+            recv_sem=sems.at[c * pieces + p],
+            device_id={"blk": wrap(b + step, n_blk)},
             device_id_type=MESH,
         )
 
@@ -288,28 +291,49 @@
             xs[blk, :, h * width : (h + 1) * width] = dot(unpack[2 * h], block).astype(BF16)
             dos[blk, :, h * width : (h + 1) * width] = dot(unpack[2 * h + 1], block).astype(BF16)
         x, do = xs[blk], dos[blk]
-        return dot_nt(x, wg_ref[0]), dot_nt(x, wu_ref[0]), dot_nt(do, wd_ref[0])
-
-    def partial_send(db):
-        values = partial(db)
-        for p in range(pieces):
-            for m, value in enumerate(values):
-                part_send[db, p, :, m * unit : (m + 1) * unit] = value[:, p * unit : (p + 1) * unit].astype(BF16)
-            rs_copy(db, p).start()
+        values = dot_nt(x, wg_ref[0]), dot_nt(x, wu_ref[0]), dot_nt(do, wd_ref[0])
+        for m, value in enumerate(values):
+            for p in range(pieces):
+                part_own[blk, p, :, m * unit : (m + 1) * unit] = value[:, p * unit : (p + 1) * unit]
 
     for fetch in fetches[4:]:
         fetch.wait()
     forward(1)
-    for m, value in enumerate(partial(0)):
-        for p in range(pieces):
-            part_own[p, :, m * unit : (m + 1) * unit] = value[:, p * unit : (p + 1) * unit]
+    partial(0)
 
     def middle(db):
         forward(db + 1)
-        partial_send(db)
+        partial(db)
 
     each(1, n_blk - 1, middle)
-    partial_send(n_blk - 1)
+    partial(n_blk - 1)
+
+    def push(c, p, step):
+        land = part_from_left if step == 1 else part_from_right
+        first = b == 0 if step == 1 else b == n_blk - 1
+
+        @pl.when(first)
+        def _():
+            part_send[c, p] = part_own[c, p].astype(BF16)
+
+        @pl.when(jnp.logical_not(first))
+        def _():
+            rs_copy(c, p, step).wait_recv()
+            part_send[c, p] = (part_own[c, p] + land[c, p].astype(F32)).astype(BF16)
+
+        rs_copy(c, p, step).start()
+
+    def to_each(p, act):
+        def one(k):
+            @pl.when(n_blk - 1 - k > b)
+            def _():
+                act(n_blk - 1 - k, p, 1)
+
+            @pl.when(k < b)
+            def _():
+                act(k, p, -1)
+
+        each(0, n_blk - 1, one)
 
     def ag_copy(c, p, to, sem):
         return pltpu.make_async_remote_copy(
@@ -336,16 +360,20 @@
         def _():
             act(to_left(p))
 
-    for p in range(pieces):
-
-        def add_part(db):
-            rs_copy(db, p).wait_recv()
-            part_own[p] += part_recv[db, p].astype(F32)
-
-        each(1, n_blk, add_part)
-        pre_gate = part_own[p, :, :unit]
-        pre_up = part_own[p, :, unit : 2 * unit]
-        dhid = part_own[p, :, 2 * unit :]
+    def settle(p):
+        @pl.when(b >= 1)
+        def _():
+            rs_copy(b, p, 1).wait_recv()
+            part_own[b, p] += part_from_left[b, p].astype(F32)
+
+        @pl.when(b + 1 < n_blk)
+        def _():
+            rs_copy(b, p, -1).wait_recv()
+            part_own[b, p] += part_from_right[b, p].astype(F32)
+
+        pre_gate = part_own[b, p, :, :unit]
+        pre_up = part_own[b, p, :, unit : 2 * unit]
+        dhid = part_own[b, p, :, 2 * unit :]
         sig = jax.nn.sigmoid(pre_gate)
         act = pre_gate * sig
         slope = sig * (1.0 + pre_gate * (1.0 - sig))
@@ -357,13 +385,12 @@
     def pass_copy(c, p, step):
         return ag_copy(c, p, wrap(b + step, n_blk), ag_s.at[c * pieces + p])
 
-    def take(c, step):
-        for p in range(pieces):
-            pass_copy(c, p, step).wait_recv()
-
-            @pl.when((b + step >= 0) & (b + step < n_blk))
-            def _():
-                pass_copy(c, p, step).start()
+    def take(c, p, step):
+        pass_copy(c, p, step).wait_recv()
+
+        @pl.when((b + step >= 0) & (b + step < n_blk))
+        def _():
+            pass_copy(c, p, step).start()
 
     def passed(c, step):
         for p in range(pieces):
@@ -380,6 +407,19 @@
         @pl.when(b + d < n_blk)
         def _():
             fn(b + d, -1)
+
+    def take_all(p):
+        each(1, n_blk, lambda d: at_distance(d, lambda c, step: take(c, p, step)))
+
+    to_each(0, push)
+    for p in range(1, pieces):
+        to_each(p, push)
+        settle(p - 1)
+        if p >= 2:
+            take_all(p - 2)
+    settle(pieces - 1)
+    if pieces >= 2:
+        take_all(pieces - 2)
 
     srow = lax.broadcasted_iota(jnp.int32, (rows, chunk), 0)
     scol = lax.broadcasted_iota(jnp.int32, (rows, chunk), 1)
@@ -453,7 +493,7 @@
     outputs(b, 0)
 
     def rest(d):
-        at_distance(d, take)
+        at_distance(d, lambda c, step: take(c, pieces - 1, step))
         at_distance(d, outputs)
         at_distance(d, finish)
 
@@ -467,7 +507,7 @@
     each(1, n_blk * n_sub, lambda k: disp_copy(k).wait_send())
     each(0, n_blk * n_sub, lambda k: fwd_copy(k).wait_send())
     for p in range(pieces):
-        each(1, n_blk, lambda db: rs_copy(db, p).wait_send())
+        to_each(p, lambda c, p, step: rs_copy(c, p, step).wait_send())
         both_ways(p, lambda copy: copy.wait_send())
     each(1, n_blk, lambda d: at_distance(d, passed))
     each(0, n_blk, lambda c: px_copy(c).wait_send())
@@ -630,7 +670,8 @@
         ((1, ff, d_blk), BF16),
         (packed, BF16),
         ((pairs * n_rep, pack, width), BF16),
-        (spread[1:], F32),
+        (spread, F32),
+        (spread, BF16),
         (spread, BF16),
         (spread, BF16),
         (packed, BF16),
@@ -646,7 +687,7 @@
         scratch_shapes=[pltpu.VMEM(shape, kind) for shape, kind in held]
         + [dma((7,))]
         + [dma((pairs,))] * 4
-        + [dma((n_blk * pieces,))] * 4
+        + [dma((n_blk * pieces,))] * 5
         + [dma((pieces,))]
         + [dma((n_blk,))] * 2
         + [dma((pairs,))] * 2,

time: 46 us -> 64.5 us (1.40)
  Pallas kernels: 45.2 us -> 63.7 us
    pallas_call x1, Pallas kernels: 41.8 us -> 60.3 us  [on_device(): pl.pallas_call(functools.partial(kernel, (n_blk, n_sub, n_rep, halves, pa...]
where the time goes in v4:
time: 64.5 us; the launch traced here: 64.4 us
  Pallas kernels  63.7 us (99%)
    pallas_call x1, Pallas kernels, on_device(): pl.pallas_call(functools.partial(kernel, (n_blk, n_sub, n_rep, halves, pa...  60.3 us
    pallas_call x1, Pallas kernels, on_device(): pl.pallas_call(functools.partial(finish_kernel, (n_blk, n_sub, halves, pa...  3.4 us

profile of v4, /device:TPU:0, one launch (start us, length us, event | category | flops | bytes accessed | tf_op | source)
XLA Modules:
  0.0 64.4 jit_solution(10432313552532074778)
XLA Ops:
  0.6 60.3 %shard_map.118 = (s32[8,128]{1,0:T(8,128)}, f32[96,128]{1,0:T(8,128)}, f32[96,128]{1,0:T(8,128)}, bf16[4,96,256]{2,1,0:T(8,128)(2,1)}, bf16[4,48,512]{2,1,0:T(8,...) custom-call(s32[8,128]{1,0:T(8,128)} %bitcast.3, ...), custom_call_target="tpu_custom_call" | custom-call | flops 1073741824 | bytes 8388608 | tf_op jit(solution)/shard_map/pallas_call | solution.py:682
  61.0 3.4 %shard_map.119 = (bf16[128,2048]{1,0:T(8,128)(2,1)}, bf16[128,2048]{1,0:T(8,128)(2,1)}, f32[8,128]{1,0:T(8,128)}, f32[1,384,512]{2,1,0:T(8,128)}, f32[1,384,512]{2,1,0:T(8,128)}, /*index=5*/f32[1,384,512]{2,1,0:T(8,128)}) custom-call(s32[8,128]{1,0:T(8,128)} %get-tuple-element.20.ids_hbm, f32[96,128]{1,0:T(8,128)} %get-tuple-element.21.sel_hbm, ...), custom_call_target="tpu_custom_call" | custom-call | flops 268435456 | bytes 5242880 | tf_op jit(solution)/shard_map/pallas_call | solution.py:710

commit v5 on v3

--- a/solution.py
+++ b/solution.py
@@ -100,6 +100,7 @@
     ag_s,
     ag_r,
     ag_l,
+    ag_far,
     px_s,
     px_r,
     bk_s,
@@ -328,6 +329,14 @@
         return ag_copy(b, p, wrap(b - 1, n_blk), ag_l.at[p])
 
     def both_ways(p, act):
+        @pl.when(b + 2 < n_blk)
+        def _():
+            act(ag_copy(b, p, wrap(b + 2, n_blk), ag_far.at[p, 0]))
+
+        @pl.when(b >= 2)
+        def _():
+            act(ag_copy(b, p, wrap(b - 2, n_blk), ag_far.at[p, 1]))
+
         @pl.when(b + 1 < n_blk)
         def _():
             act(to_right(p))
@@ -357,20 +366,29 @@
     def pass_copy(c, p, step):
         return ag_copy(c, p, wrap(b + step, n_blk), ag_s.at[c * pieces + p])
 
-    def take(c, step):
-        for p in range(pieces):
-            pass_copy(c, p, step).wait_recv()
-
-            @pl.when((b + step >= 0) & (b + step < n_blk))
-            def _():
-                pass_copy(c, p, step).start()
-
-    def passed(c, step):
-        for p in range(pieces):
-
-            @pl.when((b + step >= 0) & (b + step < n_blk))
-            def _():
-                pass_copy(c, p, step).wait_send()
+    def onward(d, step):
+        return (d >= 2) & (b + step >= 0) & (b + step < n_blk)
+
+    def take(d):
+        def one(c, step):
+            for p in range(pieces):
+                pass_copy(c, p, step).wait_recv()
+
+                @pl.when(onward(d, step))
+                def _():
+                    pass_copy(c, p, step).start()
+
+        at_distance(d, one)
+
+    def passed(d):
+        def one(c, step):
+            for p in range(pieces):
+
+                @pl.when(onward(d, step))
+                def _():
+                    pass_copy(c, p, step).wait_send()
+
+        at_distance(d, one)
 
     def at_distance(d, fn):
         @pl.when(b - d >= 0)
@@ -452,12 +470,19 @@
 
     outputs(b, 0)
 
-    def rest(d):
-        at_distance(d, take)
+    def near(d):
+        take(d)
+        take(d + 1)
         at_distance(d, outputs)
+        at_distance(d + 1, outputs)
         at_distance(d, finish)
-
-    each(1, n_blk, rest)
+        at_distance(d + 1, finish)
+
+    each(0, (n_blk - 1) // 2, lambda i: near(1 + 2 * i))
+    if n_blk % 2 == 0:
+        take(n_blk - 1)
+        at_distance(n_blk - 1, outputs)
+        at_distance(n_blk - 1, finish)
     px_copy(b).wait_recv()
     fin[b] = (px_own[b].astype(F32) + px_recv[b].astype(F32)).astype(BF16)
     each(1, n_sub, lambda ds: bk_copy(b, wrap(s + ds, n_sub)).start())
@@ -469,7 +494,7 @@
     for p in range(pieces):
         each(1, n_blk, lambda db: rs_copy(db, p).wait_send())
         both_ways(p, lambda copy: copy.wait_send())
-    each(1, n_blk, lambda d: at_distance(d, passed))
+    each(2, n_blk, passed)
     each(0, n_blk, lambda c: px_copy(c).wait_send())
     each(1, n_blk * n_sub, lambda k: bk_arrival(k).wait_send())
 
@@ -647,7 +672,7 @@
         + [dma((7,))]
         + [dma((pairs,))] * 4
         + [dma((n_blk * pieces,))] * 4
-        + [dma((pieces,))]
+        + [dma((pieces,)), dma((pieces, 2))]
         + [dma((n_blk,))] * 2
         + [dma((pairs,))] * 2,
         compiler_params=pltpu.CompilerParams(

time: 46 us -> 46.3 us (level)
  no operation moved by 1% of the time
where the time goes in v5:
time: 46.3 us; the launch traced here: 46.1 us
  Pallas kernels  45.4 us (98%)
  between operations  0.64 us (1%)
    pallas_call x1, Pallas kernels, on_device(): pl.pallas_call(functools.partial(kernel, (n_blk, n_sub, n_rep, halves, pa...  42 us
    pallas_call x1, Pallas kernels, on_device(): pl.pallas_call(functools.partial(finish_kernel, (n_blk, n_sub, halves, pa...  3.39 us

profile of v5, /device:TPU:0, one launch (start us, length us, event | category | flops | bytes accessed | tf_op | source)
XLA Modules:
  0.0 46.1 jit_solution(16548211944407059723)
XLA Ops:
  0.6 42.0 %shard_map.118 = (s32[8,128]{1,0:T(8,128)}, f32[96,128]{1,0:T(8,128)}, f32[96,128]{1,0:T(8,128)}, bf16[4,96,256]{2,1,0:T(8,128)(2,1)}, bf16[4,48,512]{2,1,0:T(8,...) custom-call(s32[8,128]{1,0:T(8,128)} %bitcast.3, ...), custom_call_target="tpu_custom_call" | custom-call | flops 1073741824 | bytes 8388608 | tf_op jit(solution)/shard_map/pallas_call | solution.py:666
  42.7 3.4 %shard_map.119 = (bf16[128,2048]{1,0:T(8,128)(2,1)}, bf16[128,2048]{1,0:T(8,128)(2,1)}, f32[8,128]{1,0:T(8,128)}, f32[1,384,512]{2,1,0:T(8,128)}, f32[1,384,512]{2,1,0:T(8,128)}, /*index=5*/f32[1,384,512]{2,1,0:T(8,128)}) custom-call(s32[8,128]{1,0:T(8,128)} %get-tuple-element.20.ids_hbm, f32[96,128]{1,0:T(8,128)} %get-tuple-element.21.sel_hbm, ...), custom_call_target="tpu_custom_call" | custom-call | flops 268435456 | bytes 5242880 | tf_op jit(solution)/shard_map/pallas_call | solution.py:694

commit v6 on v5

--- a/solution.py
+++ b/solution.py
@@ -100,7 +100,6 @@
     ag_s,
     ag_r,
     ag_l,
-    ag_far,
     px_s,
     px_r,
     bk_s,
@@ -329,14 +328,6 @@
         return ag_copy(b, p, wrap(b - 1, n_blk), ag_l.at[p])
 
     def both_ways(p, act):
-        @pl.when(b + 2 < n_blk)
-        def _():
-            act(ag_copy(b, p, wrap(b + 2, n_blk), ag_far.at[p, 0]))
-
-        @pl.when(b >= 2)
-        def _():
-            act(ag_copy(b, p, wrap(b - 2, n_blk), ag_far.at[p, 1]))
-
         @pl.when(b + 1 < n_blk)
         def _():
             act(to_right(p))
@@ -366,29 +357,30 @@
     def pass_copy(c, p, step):
         return ag_copy(c, p, wrap(b + step, n_blk), ag_s.at[c * pieces + p])
 
-    def onward(d, step):
-        return (d >= 2) & (b + step >= 0) & (b + step < n_blk)
+    def onward(step):
+        return (b + step >= 0) & (b + step < n_blk)
 
     def take(d):
-        def one(c, step):
-            for p in range(pieces):
+        for p in range(pieces):
+
+            def one(c, step):
                 pass_copy(c, p, step).wait_recv()
 
-                @pl.when(onward(d, step))
+                @pl.when(onward(step))
                 def _():
                     pass_copy(c, p, step).start()
 
-        at_distance(d, one)
+            at_distance(d, one)
 
     def passed(d):
-        def one(c, step):
-            for p in range(pieces):
-
-                @pl.when(onward(d, step))
+        for p in range(pieces):
+
+            def one(c, step):
+                @pl.when(onward(step))
                 def _():
                     pass_copy(c, p, step).wait_send()
 
-        at_distance(d, one)
+            at_distance(d, one)
 
     def at_distance(d, fn):
         @pl.when(b - d >= 0)
@@ -494,7 +486,7 @@
     for p in range(pieces):
         each(1, n_blk, lambda db: rs_copy(db, p).wait_send())
         both_ways(p, lambda copy: copy.wait_send())
-    each(2, n_blk, passed)
+    each(1, n_blk, passed)
     each(0, n_blk, lambda c: px_copy(c).wait_send())
     each(1, n_blk * n_sub, lambda k: bk_arrival(k).wait_send())
 
@@ -672,7 +664,7 @@
         + [dma((7,))]
         + [dma((pairs,))] * 4
         + [dma((n_blk * pieces,))] * 4
-        + [dma((pieces,)), dma((pieces, 2))]
+        + [dma((pieces,))]
         + [dma((n_blk,))] * 2
         + [dma((pairs,))] * 2,
         compiler_params=pltpu.CompilerParams(

time: 46.3 us -> 44.4 us (0.959)
  Pallas kernels: 45.4 us -> 43.6 us
    pallas_call x1, Pallas kernels: 42 us -> 40.2 us  [on_device(): pl.pallas_call(functools.partial(kernel, (n_blk, n_sub, n_rep, halves, pa...]
where the time goes in v6:
time: 44.4 us; the launch traced here: 44.2 us
  Pallas kernels  43.6 us (98%)
  between operations  0.64 us (1%)
    pallas_call x1, Pallas kernels, on_device(): pl.pallas_call(functools.partial(kernel, (n_blk, n_sub, n_rep, halves, pa...  40.2 us
    pallas_call x1, Pallas kernels, on_device(): pl.pallas_call(functools.partial(finish_kernel, (n_blk, n_sub, halves, pa...  3.4 us

profile of v6, /device:TPU:0, one launch (start us, length us, event | category | flops | bytes accessed | tf_op | source)
XLA Modules:
  0.0 44.2 jit_solution(13119008244892255036)
XLA Ops:
  0.6 40.2 %shard_map.118 = (s32[8,128]{1,0:T(8,128)}, f32[96,128]{1,0:T(8,128)}, f32[96,128]{1,0:T(8,128)}, bf16[4,96,256]{2,1,0:T(8,128)(2,1)}, bf16[4,48,512]{2,1,0:T(8,...) custom-call(s32[8,128]{1,0:T(8,128)} %bitcast.3, ...), custom_call_target="tpu_custom_call" | custom-call | flops 1073741824 | bytes 8388608 | tf_op jit(solution)/shard_map/pallas_call | solution.py:658
  40.8 3.4 %shard_map.119 = (bf16[128,2048]{1,0:T(8,128)(2,1)}, bf16[128,2048]{1,0:T(8,128)(2,1)}, f32[8,128]{1,0:T(8,128)}, f32[1,384,512]{2,1,0:T(8,128)}, f32[1,384,512]{2,1,0:T(8,128)}, /*index=5*/f32[1,384,512]{2,1,0:T(8,128)}) custom-call(s32[8,128]{1,0:T(8,128)} %get-tuple-element.20.ids_hbm, f32[96,128]{1,0:T(8,128)} %get-tuple-element.21.sel_hbm, ...), custom_call_target="tpu_custom_call" | custom-call | flops 268435456 | bytes 5242880 | tf_op jit(solution)/shard_map/pallas_call | solution.py:686

commit v7 on v6

--- a/solution.py
+++ b/solution.py
@@ -268,8 +268,6 @@
             acc = term if acc is None else acc + term
         cots[blk] = acc.astype(BF16)
 
-    each(0, n_blk, cot_rows)
-
     def rs_copy(db, p):
         return pltpu.make_async_remote_copy(
             src_ref=part_send.at[db, p],
@@ -461,6 +459,7 @@
         each(0, n_sub, lambda dst_s: bk_copy(c, dst_s).start())
 
     outputs(b, 0)
+    each(0, n_blk, cot_rows)
 
     def near(d):
         take(d)

time: 44.4 us -> 44.4 us (level)
  no operation moved by 1% of the time
where the time goes in v7:
time: 44.4 us; the launch traced here: 44.2 us
  Pallas kernels  43.6 us (98%)
  between operations  0.64 us (1%)
    pallas_call x1, Pallas kernels, on_device(): pl.pallas_call(functools.partial(kernel, (n_blk, n_sub, n_rep, halves, pa...  40.2 us
    pallas_call x1, Pallas kernels, on_device(): pl.pallas_call(functools.partial(finish_kernel, (n_blk, n_sub, halves, pa...  3.4 us

profile of v7, /device:TPU:0, one launch (start us, length us, event | category | flops | bytes accessed | tf_op | source)
XLA Modules:
  0.0 44.2 jit_solution(1900512908945570569)
XLA Ops:
  0.6 40.2 %shard_map.118 = (s32[8,128]{1,0:T(8,128)}, f32[96,128]{1,0:T(8,128)}, f32[96,128]{1,0:T(8,128)}, bf16[4,96,256]{2,1,0:T(8,128)(2,1)}, bf16[4,48,512]{2,1,0:T(8,...) custom-call(s32[8,128]{1,0:T(8,128)} %bitcast.3, ...), custom_call_target="tpu_custom_call" | custom-call | flops 1073741824 | bytes 8388608 | tf_op jit(solution)/shard_map/pallas_call | solution.py:657
  40.8 3.4 %shard_map.119 = (bf16[128,2048]{1,0:T(8,128)(2,1)}, bf16[128,2048]{1,0:T(8,128)(2,1)}, f32[8,128]{1,0:T(8,128)}, f32[1,384,512]{2,1,0:T(8,128)}, f32[1,384,512]{2,1,0:T(8,128)}, /*index=5*/f32[1,384,512]{2,1,0:T(8,128)}) custom-call(s32[8,128]{1,0:T(8,128)} %get-tuple-element.20.ids_hbm, f32[96,128]{1,0:T(8,128)} %get-tuple-element.21.sel_hbm, ...), custom_call_target="tpu_custom_call" | custom-call | flops 268435456 | bytes 5242880 | tf_op jit(solution)/shard_map/pallas_call | solution.py:685
